TPU v7x, 512 devices: a whole 4x8x8 slice. The times are simulated.
512 devices in a mesh: row: 32 (over y, x), col: 16 (over z, core).
Axes of the slice: x: 4, y: 8, z: 8, core: 2. Of those that a mesh axis runs over, the one named last changes fastest.
Arguments:
- transition: float32 [16384, 16384], P('row', 'col'), may hold values from 0.1 to 10
- alphas: float32 [2, 256, 16384], P(None, 'col', 'row'), may hold values from 0.1 to 10
- beta_last: float32 [256, 16384], P('col', 'row'), may hold values from 0.1 to 10
- emission: float32 [128, 16384], P(None, 'row'), may hold values from 0.05 to 1
- token_ids: int32 [2, 256], P(None, 'col'), may hold values from 0 to 127
Outputs:
- beta_first: float32 [256, 16384], P('col', 'row')
- counts: float32 [16384, 16384], P('row', 'col')
All inputs are finite; a program needn't handle non-finite values.
Results may differ from a plain program's by a relative error of at most 0.0001.
Values sent between devices are 32-bit elements; how exact they have to be, the bound alone decides.
A program may use at most 64 MiB of HBM per device.

v0:
```python
import jax
import jax.numpy as jnp
from jax import lax
from jax.sharding import PartitionSpec as P

H = 16384
STEPS = 2


def contract_seq(scaled, columns):
    return lax.dot_general(
        scaled,
        columns,
        (((0,), (0,)), ((), ())),
        precision=lax.Precision.HIGHEST,
        preferred_element_type=jnp.float32,
    )


def per_device(transition, alphas, beta_last, emission, token_ids):
    blocks = beta_last.shape[0]
    ncols = emission.shape[0]
    seqs = blocks * lax.axis_size("col")
    factor = float(H * H) / float(seqs * STEPS)
    labels = lax.broadcasted_iota(jnp.int32, (blocks, ncols), 1)
    beta = beta_last
    total = jnp.zeros(transition.shape, jnp.float32)
    for k in range(STEPS):
        onehot = (token_ids[k][:, None] == labels).astype(jnp.float32)
        emit = jnp.dot(
            onehot, emission, precision=lax.Precision.HIGHEST, preferred_element_type=jnp.float32
        )
        weighted = emit * beta
        panel = lax.all_gather(weighted, "row", axis=1, tiled=True)
        columns = lax.all_to_all(panel, "col", split_axis=1, concat_axis=0, tiled=True)
        local = lax.psum_scatter(
            lax.dot_general(
                columns,
                transition,
                (((1,), (1,)), ((), ())),
                precision=lax.Precision.HIGHEST,
                preferred_element_type=jnp.float32,
            ),
            "col",
            scatter_dimension=0,
            tiled=True,
        )
        norms = lax.psum(jnp.sum(alphas[k] * local, axis=1), "row")
        beta = local / norms[:, None] * H
        scaled = lax.all_gather(alphas[k] / norms[:, None], "col", axis=0, tiled=True)
        total = total + contract_seq(scaled, columns)
    counts = transition * total * factor
    return (beta, counts)


def solution(mesh):
    return jax.shard_map(
        per_device,
        mesh=mesh,
        in_specs=(
            P("row", "col"),
            P(None, "col", "row"),
            P("col", "row"),
            P(None, "row"),
            P(None, "col"),
        ),
        out_specs=(P("col", "row"), P("row", "col")),
        check_vma=False,
    )
```

profile of v0, /device:TPU:1, one launch (start us, length us, event | category | flops | bytes accessed | tf_op | source)
XLA Modules:
  0.0 560.8 jit_solution(10932562394011031633)
XLA Ops:
  7.2 0.0 copy-start
  7.2 0.0 all-gather.3.cloned.1.call-start
  7.2 0.8 slice_bitcast_fusion.1
  8.0 0.1 copy-done
  8.1 1.6 convolution_multiply_fusion
  9.7 0.0 all-gather.3.cloned.1.call-update
  9.7 0.0 reduce-scatter.3.cloned.1.call-start
  9.8 84.5 %all-gather.3.cloned.1.call-done = f32[16,16384]{1,0:T(8,128)} async-done(((f32[16,512]{1,0:T(8,128)}), f32[16,16384]{1,0:T(8,128)}) %all-gather.3.cloned.1.call-update) | async-done | bytes 1048592 | tf_op jit(solution)/shard_map/all_gather | solution.py:34
  94.3 0.0 copy-start.1
  94.3 1.5 copy.14
  95.8 40.8 %all_to_all.38 = f32[16,16,1024]{2,0,1:T(8,128)S(1)} all-to-all(f32[16,16,1024]{2,0,1:T(8,128)S(1)} %bitcast.42), channel_id=1, replica_groups=mesh['row'=32,'col'=16] {'col'}, dimensions={1} | all-to-all | bytes 2097152 | tf_op jit(solution)/shard_map/all_to_all | solution.py:35
  136.5 0.0 copy-done.1
  136.5 0.0 copy-start.4
  136.5 2.7 fusion.4
  139.3 0.0 reduce-scatter.3.cloned.1.call-update
  139.3 0.0 all-gather.5.cloned.1.call-start
  139.3 50.1 %reduce-scatter.3.cloned.1.call-done = f32[16,512]{1,0:T(8,128)} async-done(((f32[256,512]{1,0:T(8,128)}), f32[16,512]{1,0:T(8,128)}) %reduce-scatter.3.cloned.1.call-update) | async-done | bytes 32784 | tf_op jit(solution)/shard_map/reduce_scatter | solution.py:36
  189.5 0.0 copy-done.4
  189.5 0.9 fusion.1
  190.4 60.6 %psum.14 = f32[16]{0:T(128)S(1)} all-reduce(f32[16]{0:T(128)S(1)} %fusion.1), channel_id=1, replica_groups=mesh['row'=32,'col'=16] {'row'}, use_global_device_ids=true, to_apply=%region_2.0 | all-reduce | flops 16 | bytes 128 | tf_op jit(solution)/shard_map/psum | solution.py:48
  251.0 1.6 convolution_multiply_fusion.1
  252.6 0.0 all-gather.5.cloned.1.call-update
  252.6 0.0 reduce-scatter.5.cloned.1.call-start
  252.7 86.9 %all-gather.5.cloned.1.call-done = f32[16,16384]{1,0:T(8,128)} async-done(((f32[16,512]{1,0:T(8,128)}), f32[16,16384]{1,0:T(8,128)}) %all-gather.5.cloned.1.call-update) | async-done | bytes 1048592 | tf_op jit(solution)/shard_map/all_gather | solution.py:34
  339.5 1.3 copy.13
  340.9 40.8 %all_to_all.39 = f32[16,16,1024]{2,0,1:T(8,128)S(1)} all-to-all(f32[16,16,1024]{2,0,1:T(8,128)S(1)} %bitcast.43), channel_id=1, replica_groups=mesh['row'=32,'col'=16] {'col'}, dimensions={1} | all-to-all | bytes 2097152 | tf_op jit(solution)/shard_map/all_to_all | solution.py:35
  381.6 0.0 copy-start.2
  381.6 1.0 copy-done.2
  382.6 2.7 fusion.5
  385.3 0.0 reduce-scatter.5.cloned.1.call-update
  385.4 50.2 %reduce-scatter.5.cloned.1.call-done = f32[16,512]{1,0:T(8,128)} async-done(((f32[256,512]{1,0:T(8,128)}), f32[16,512]{1,0:T(8,128)}) %reduce-scatter.5.cloned.1.call-update) | async-done | bytes 32784 | tf_op jit(solution)/shard_map/reduce_scatter | solution.py:36
  435.5 0.9 fusion
  436.4 60.7 %psum.15 = f32[16]{0:T(128)S(1)} all-reduce(f32[16]{0:T(128)S(1)} %fusion), channel_id=1, replica_groups=mesh['row'=32,'col'=16] {'row'}, use_global_device_ids=true, to_apply=%region_5.0 | all-reduce | flops 16 | bytes 128 | tf_op jit(solution)/shard_map/psum | solution.py:48
  497.1 1.5 bitcast_divide_fusion
  498.5 33.0 %all_gather.14 = f32[256,512]{1,0:T(8,128)S(1)} all-gather(f32[16,512]{1,0:T(8,128)S(1)} %get-tuple-element.3), channel_id=1, replica_groups=mesh['row'=32,'col'=16] {'col'}, dimensions={0}, use_global_device_ids=true | all-gather | bytes 557056 | tf_op jit(solution)/shard_map/all_gather | solution.py:50
  531.5 0.0 copy-start.3
  531.5 1.9 fusion.6
  533.3 17.4 %all_gather.15 = f32[256,512]{1,0:T(8,128)S(1)} all-gather(f32[16,512]{1,0:T(8,128)S(1)} %get-tuple-element.2), channel_id=1, replica_groups=mesh['row'=32,'col'=16] {'col'}, dimensions={0}, use_global_device_ids=true | all-gather | bytes 557056 | tf_op jit(solution)/shard_map/all_gather | solution.py:50
  550.8 0.0 copy-done.3
  550.8 3.5 multiply_multiply_fusion
Async XLA Ops:
  7.2 1.0 copy-start
  7.2 87.1 %all-gather.3.cloned.1.call-start = ((), (), s32[]{:S(2)}) async-start(), calls=%async_computation.4 | async-start | bytes 1081344 | tf_op jit(solution)/shard_map/all_gather | solution.py:34
  9.7 179.7 %reduce-scatter.3.cloned.1.call-start = ((), (), s32[]{:S(2)}) async-start(), calls=%async_computation.5 | async-start | bytes 557056 | tf_op jit(solution)/shard_map/reduce_scatter | solution.py:36
  94.3 42.2 %copy-start.1 = (f32[512,1024]{1,0:T(8,128)S(1)}, f32[512,1024]{1,0:T(8,128)}, u32[]{:S(2)}) copy-start(f32[512,1024]{1,0:T(8,128)} %param.5) | copy-start | bytes 6291460
  136.5 53.0 %copy-start.4 = (f32[2,16,512]{2,1,0:T(8,128)S(1)}, f32[2,16,512]{2,1,0:T(8,128)}, u32[]{:S(2)}) copy-start(f32[2,16,512]{2,1,0:T(8,128)} %param.6) | copy-start | bytes 196612
  139.3 200.3 %all-gather.5.cloned.1.call-start = ((), (), s32[]{:S(2)}) async-start(), calls=%async_computation.6 | async-start | bytes 1081344 | tf_op jit(solution)/shard_map/all_gather | solution.py:34
  252.6 182.9 %reduce-scatter.5.cloned.1.call-start = ((), (), s32[]{:S(2)}) async-start(), calls=%async_computation.7 | async-start | bytes 557056 | tf_op jit(solution)/shard_map/reduce_scatter | solution.py:36
  381.6 1.0 copy-start.2
  531.5 19.3 %copy-start.3 = (f32[16,16,1024]{2,0,1:T(8,128)S(1)}, f32[16,16,1024]{2,0,1:T(8,128)}, u32[]{:S(2)}) copy-start(f32[16,16,1024]{2,0,1:T(8,128)} %copy-done.2) | copy-start | bytes 3145732
Sparse Core Ops, SparseCore 0:
  11.8 82.4 all-gather.2
  139.4 50.0 reduce-scatter.2
  252.7 86.7 all-gather.4
  385.5 50.0 reduce-scatter.4
where the time goes:
time: 561 us
  waiting for transfers between devices  272 us (48%)
  blocking collectives  253 us (45%)
  matrix products  14 us (2%)
  between operations  13.8 us (2%)
    all_gather x2, waiting for transfers between devices, per_device(): panel = lax.all_gather(weighted, 'row', axis=1, tiled=True)  171 us
    psum x2, blocking collectives, per_device(): norms = lax.psum(jnp.sum(alphas[k] * local, axis=1), 'row')  121 us
    reduce_scatter x2, waiting for transfers between devices, per_device(): lax.psum_scatter(lax.dot_general(columns, transition, (((1,), (1,)), ((),...  100 us
    all_to_all x2, blocking collectives, per_device(): lax.all_to_all(panel, 'col', split_axis=1, concat_axis=0, tiled=True)  81.5 us
    all_gather x2, blocking collectives, per_device(): lax.all_gather(alphas[k] / norms[:, None], 'col', axis=0, tiled=True)  50.4 us
  transfers between devices with their start and end apart: 4, of which 4 were waited for; matrix products, arithmetic and copies ran while one was open for 0% of the time, Pallas kernels for 0%

commit v1 on v0

v1 whole, which is shorter than its diff:
```python
import functools

import jax
import jax.numpy as jnp
from jax import lax
from jax.experimental import pallas as pl
from jax.experimental.pallas import tpu as pltpu
from jax.sharding import PartitionSpec as P

H = 16384
STEPS = 2
SEQ = 256
X, Y, Z, C = 4, 8, 8, 2
BS = SEQ // (Z * C)
HALF = BS * Z
RB = H // (X * Y)
CB = H // (Z * C)
NCOL = 128
FACTOR = float(H * H) / float(SEQ * STEPS)
F32 = jnp.float32
BF16 = jnp.bfloat16
MESH = pl.DeviceIdType.MESH


def loop(n, body, start=0):
    def step(i, carry):
        body(i)
        return carry

    lax.fori_loop(start, n, step, 0)


def remote(src, dst, send, recv, row, col):
    return pltpu.make_async_remote_copy(
        src_ref=src, dst_ref=dst, send_sem=send, recv_sem=recv, device_id=(row, col), device_id_type=MESH
    )


def wait(ref, sem):
    pltpu.make_async_copy(ref, ref, sem).wait()


def near_first(j):
    return (j % 2) * ((j + 1) // 2) + (1 - j % 2) * (8 - j // 2)


def split(v):
    hi = v.astype(BF16)
    return hi, (v - hi.astype(F32)).astype(BF16)


def dot(a, b, dims):
    return lax.dot_general(a, b, (dims, ((), ())), preferred_element_type=F32)


NT = ((1,), (1,))
NN = ((1,), (0,))


def kernel(
    trans_hbm, alphas_hbm, beta_hbm, emis_hbm, tok_ref,
    beta_out, counts_hbm,
    t_f, t_hi, t_lo, emis, beta0, al, at_hi, at_lo, tsend, tw, wblk, w, ub, pr, cr, tot, outb, zz, zy, zx, zp, zc,
    ld, t_s, t_r, a_s, a_r, ap, y_s, y_r, x_s, x_r, f_s, p_s, p_r, c_s, c_r, zz_s, zz_r, zy_s, zy_r, zx_s, zx_r, zp_s, zp_r, o_s,
):
    row = lax.axis_index("row")
    col = lax.axis_index("col")
    x, y, z, k = row % X, row // X, col // C, col % C
    kd = x // 2
    slot = x % 2
    q = (x - 2 * k + 4) % 4
    fslot = 1 - slot
    fhalf = q // 2
    fplus = ((q + 1) // 2) % 2
    xp, xm = (x + 1) % X, (x + X - 1) % X
    fx = fplus * xp + (1 - fplus) * xm
    other = z * C + 1 - k

    loads = [
        pltpu.make_async_copy(emis_hbm, emis, ld.at[0]),
        pltpu.make_async_copy(beta_hbm, beta0, ld.at[1]),
        pltpu.make_async_copy(alphas_hbm, al.at[:, pl.ds(k * HALF + z * BS, BS)], ld.at[2]),
        pltpu.make_async_copy(trans_hbm, t_f, ld.at[3]),
    ]
    for c in loads:
        c.start()

    bar = pltpu.get_barrier_semaphore()

    def greet(r, c):
        pl.semaphore_signal(bar, inc=1, device_id=(r, c), device_id_type=MESH)

    def greet_lines(d):
        greet(row, ((z + d) % Z) * C + k)
        greet(((y + d) % Y) * X + x, col)
        greet(((y + d) % Y) * X + x, other)

    loop(Z, greet_lines, 1)
    loop(X, lambda d: greet(y * X + (x + d) % X, col), 1)
    greet(row, other)

    @pl.when(y != z)
    def _():
        def greet_cross(d):
            greet(((y + d) % Y) * X + x, y * C + k)

            @pl.when((z + d) % Z != y)
            def _():
                greet(z * X + x, ((z + d) % Z) * C + k)

        loop(Z, greet_cross, 1)

    loads[0].wait()
    labels = lax.broadcasted_iota(jnp.int32, (NCOL, BS), 0)
    em = emis[...]

    def emit(step):
        onehot = (labels == tok_ref[step : step + 1, :]).astype(F32)
        return lax.dot_general(
            onehot, em, (((0,), (0,)), ((), ())), precision=lax.Precision.HIGHEST, preferred_element_type=F32
        )

    loads[1].wait()
    tsend[0] = emit(0) * beta0[...]
    tsend[1] = emit(1)

    apart = ((y - z + Z) % Z + Z - 1) // Z
    pl.semaphore_wait(bar, 3 * (Z - 1) + X + apart * (2 * Z - 3))

    for i in range(2):
        @pl.when(y != z)
        def _():
            remote(tsend.at[i], tw.at[i], t_s.at[i], t_r.at[i], z * X + x, y * C + k).start()

        @pl.when(y == z)
        def _():
            pltpu.make_async_copy(tsend.at[i], tw.at[i], t_r.at[i]).start()

    loads[2].wait()
    mine = al.at[:, pl.ds(k * HALF + z * BS, BS)]

    def alpha_send(d):
        remote(mine, mine, a_s.at[d], a_r.at[z], row, ((z + d) % Z) * C + k).start()

    loop(Z, alpha_send, 1)

    def rows(g, s):
        return pl.ds(g * HALF + s * BS, BS)

    def y_sends(step, src):
        dst = w.at[step, slot, rows(k, y)]

        @pl.when(k == kd)
        def _():
            pltpu.make_async_copy(src, dst, y_r.at[step, k, y]).start()

        @pl.when(k != kd)
        def _():
            remote(src, dst, y_s.at[step, 0], y_r.at[step, k, y], row, other).start()

        def send(j):
            to = (y + near_first(j)) % Y
            remote(src, dst, y_s.at[step, j], y_r.at[step, k, y], to * X + x, z * C + kd).start()

        loop(Y, send, 1)

    def x_sends(step, g):
        @pl.when(k == kd)
        def _():
            def send(j):
                s = (y + near_first(j)) % Y
                ref = w.at[step, slot, rows(g, s)]
                wait(ref, y_r.at[step, g, s])
                remote(ref, ref, x_s.at[step, 0, g, j], x_r.at[step, slot, g, s], y * X + xp, col).start()
                remote(ref, ref, x_s.at[step, 1, g, j], x_r.at[step, slot, g, s], y * X + xm, col).start()

            loop(Y, send)

    def forwards(step, g):
        def send(i):
            s = (y + near_first(2 * i + fhalf)) % Y
            ref = w.at[step, fslot, rows(g, s)]
            wait(ref, x_r.at[step, fslot, g, s])
            remote(ref, ref, f_s.at[step, g, i], x_r.at[step, fslot, g, s], y * X + fx, col).start()

        loop(Y // 2, send)

    def arrivals(step, g):
        def rest(i):
            s = (y + near_first(2 * i + 1 - fhalf)) % Y
            wait(w.at[step, fslot, rows(g, s)], x_r.at[step, fslot, g, s])

        loop(Y // 2, rest)

        @pl.when(k != kd)
        def _():
            def full(s):
                wait(w.at[step, slot, rows(g, s)], x_r.at[step, slot, g, s])

            loop(Y, full)

    def z_sum(buf, n):
        v = buf[0]
        for i in range(1, n):
            v = v + buf[i]
        return v

    def z_first(step, prod):
        part = prod[:, 0:128]
        for i in range(1, RB // 128):
            part = part + prod[:, i * 128 : (i + 1) * 128]
        zz[step, z] = jnp.broadcast_to(jnp.sum(jnp.transpose(part), axis=0, keepdims=True), (8, HALF))

        def send(d):
            ref = zz.at[step, z]
            remote(ref, ref, zz_s.at[step, d], zz_r.at[step, z], row, ((z + d) % Z) * C + k).start()

        loop(Z, send, 1)

    def z_second(step):
        loop(Z, lambda d: wait(zz.at[step, (z + d) % Z], zz_r.at[step, (z + d) % Z]), 1)
        zy[step, y] = z_sum(zz.at[step], Z)

        def send(d):
            ref = zy.at[step, y]
            remote(ref, ref, zy_s.at[step, d], zy_r.at[step, y], ((y + d) % Y) * X + x, col).start()

        loop(Y, send, 1)

    def z_third(step):
        loop(Y, lambda d: wait(zy.at[step, (y + d) % Y], zy_r.at[step, (y + d) % Y]), 1)
        zx[step, x] = z_sum(zy.at[step], Y)

        def send(d):
            ref = zx.at[step, x]
            remote(ref, ref, zx_s.at[step, d], zx_r.at[step, x], y * X + (x + d) % X, col).start()

        loop(X, send, 1)

    def z_fourth(step):
        loop(X, lambda d: wait(zx.at[step, (x + d) % X], zx_r.at[step, (x + d) % X]), 1)
        zp[step, k] = z_sum(zx.at[step], X)
        ref = zp.at[step, k]
        remote(ref, ref, zp_s.at[step], zp_r.at[step], row, other).start()

    def z_last(step):
        wait(zp.at[step, 1 - k], zp_r.at[step])
        for g in range(C):
            zc[step, g] = jnp.transpose(jnp.broadcast_to(zp[step, g, 0:1, :], (HALF, HALF)))

    def product(step, g):
        acc = None
        for sl in range(2):
            hi, lo = split(w[step, sl, g * HALF : (g + 1) * HALF, :])
            cols = slice(sl * RB, (sl + 1) * RB)
            both = dot(jnp.concatenate([hi, lo], axis=0), t_hi[:, cols], NT)
            part = both[:HALF] + both[HALF:] + dot(hi, t_lo[:, cols], NT)
            acc = part if acc is None else acc + part
        ub[step, g] = acc

        @pl.when(k != g)
        def _():
            remote(ub.at[step, g], pr.at[step], p_s.at[step], p_r.at[step], row, other).start()

        @pl.when(k == g)
        def _():
            wait(pr.at[step], p_r.at[step])
            u = ub[step, g] + pr[step]
            ub[step, g] = u

            def send(d):
                if step == 0:
                    s = (y + d) % Y
                    r, c = s * X + x, y * C + k
                else:
                    s = (z + d) % Z
                    r, c = row, s * C + k
                src = ub.at[step, g, pl.ds(s * BS, BS)]
                remote(src, cr.at[step, z], c_s.at[step, d], c_r.at[step, z], r, c).start()

            loop(Z, send, 1)
            if step == 0:
                src = ub.at[step, g, pl.ds(y * BS, BS)]

                @pl.when(y != z)
                def _():
                    remote(src, cr.at[step, z], c_s.at[step, 0], c_r.at[step, z], row, y * C + k).start()

                @pl.when(y == z)
                def _():
                    pltpu.make_async_copy(src, cr.at[step, z], c_r.at[step, z]).start()

                loop(Z, lambda d: wait(al.at[:, pl.ds(k * HALF + ((z + d) % Z) * BS, BS)], a_r.at[(z + d) % Z]), 1)
                half = al.at[:, pl.ds(k * HALF, HALF)]
                remote(half, half, ap.at[0], ap.at[1], row, other).start()
            else:
                src = ub.at[step, g, pl.ds(z * BS, BS)]
                pltpu.make_async_copy(src, cr.at[step, z], c_r.at[step, z]).start()
            z_first(step, u * al[step, pl.ds(k * HALF, HALF), :])

    def reduced(step):
        acc = None
        for i in range(Z):
            wait(cr.at[step, i], c_r.at[step, i])
            acc = cr[step, i] if acc is None else acc + cr[step, i]
        return acc

    def next_weighted(g):
        @pl.when(k == g)
        def _():
            wblk[...] = reduced(0) * tw[1]
            y_sends(1, wblk)

    def scaled_columns(step, sl):
        parts = []
        for g in range(C):
            inv = 1.0 / zc[step, g]
            parts.append(w[step, sl, g * HALF : (g + 1) * HALF, :] * jnp.concatenate([inv] * (RB // HALF), axis=1))
        return split(jnp.concatenate(parts, axis=0))

    def counts_part(step, hi, lo, r):
        return (
            dot(at_hi[step, r, :], hi, NN) + dot(at_lo[step, r, :], hi, NN) + dot(at_hi[step, r, :], lo, NN)
        )

    wait(tw.at[0], t_r.at[0])
    y_sends(0, tw.at[0])
    loads[3].wait()

    def split_rows(i):
        r = pl.ds(pl.multiple_of(i * 64, 64), 64)
        hi, lo = split(t_f[r, :])
        t_hi[r, :] = hi
        t_lo[r, :] = lo

    loop(RB // 64, split_rows)
    wait(tw.at[1], t_r.at[1])
    x_sends(0, 0)
    x_sends(0, 1)
    forwards(0, 0)
    arrivals(0, 0)
    product(0, 0)
    forwards(0, 1)
    arrivals(0, 1)
    product(0, 1)

    next_weighted(0)
    z_second(0)
    x_sends(1, 0)
    next_weighted(1)
    forwards(1, 0)
    z_third(0)
    wait(al.at[:, pl.ds((1 - k) * HALF, HALF)], ap.at[1])
    for step in range(STEPS):
        for i in range(RB // 128):
            hi, lo = split(jnp.transpose(al[step, :, i * 128 : (i + 1) * 128]))
            at_hi[step, i * 128 : (i + 1) * 128, :] = hi
            at_lo[step, i * 128 : (i + 1) * 128, :] = lo
    z_fourth(0)
    x_sends(1, 1)
    z_last(0)
    for sl in range(2):
        hi, lo = scaled_columns(0, sl)
        tot[:, sl * RB : (sl + 1) * RB] = counts_part(0, hi, lo, slice(None))
    arrivals(1, 0)
    product(1, 0)
    forwards(1, 1)
    arrivals(1, 1)
    product(1, 1)

    z_second(1)
    z_third(1)
    z_fourth(1)
    z_last(1)
    for sl in range(2):
        hi, lo = scaled_columns(1, sl)
        cols = slice(sl * RB, (sl + 1) * RB)
        outb[:, cols] = (t_f[:, cols] * (tot[:, cols] + counts_part(1, hi, lo, slice(None)))) * FACTOR
        pltpu.make_async_copy(outb.at[:, cols], counts_hbm.at[:, cols], o_s.at[sl]).start()
    norm = zc[1, k, pl.ds(pl.multiple_of(z * BS, BS), BS), :]
    beta_out[...] = (reduced(1) / jnp.concatenate([norm] * (RB // HALF), axis=1)) * float(H)

    @pl.when(y != z)
    def _():
        wait(tsend.at[0], t_s.at[0])
        wait(tsend.at[1], t_s.at[1])
        wait(cr.at[0, 0], c_s.at[0, 0])

    @pl.when(k != kd)
    def _():
        wait(wblk, y_s.at[0, 0])
        wait(wblk, y_s.at[1, 0])

    @pl.when(k == kd)
    def _():
        for step in range(STEPS):
            def sent(j):
                for g in range(C):
                    for d in range(2):
                        wait(wblk, x_s.at[step, d, g, j])

            loop(Y, sent)

    def sent_lines(d):
        wait(mine, a_s.at[d])
        for step in range(STEPS):
            wait(wblk, y_s.at[step, d])
            wait(wblk, c_s.at[step, d])
            wait(zz.at[0, 0], zz_s.at[step, d])
            wait(zz.at[0, 0], zy_s.at[step, d])

    loop(Z, sent_lines, 1)
    wait(al.at[:, pl.ds(0, HALF)], ap.at[0])
    for step in range(STEPS):
        wait(pr.at[0], p_s.at[step])
        wait(zz.at[0, 0], zp_s.at[step])
        loop(X, lambda d: wait(zz.at[0, 0], zx_s.at[step, d]), 1)

        def sent_on(i):
            for g in range(C):
                wait(wblk, f_s.at[step, g, i])

        loop(Y // 2, sent_on)
    for sl in range(2):
        cols = slice(sl * RB, (sl + 1) * RB)
        wait(outb.at[:, cols], o_s.at[sl])


def per_device(transition, alphas, beta_last, emission, token_ids):
    anywhere = pl.BlockSpec(memory_space=pl.ANY)
    vmem = pl.BlockSpec(memory_space=pltpu.VMEM)
    dma = pltpu.SemaphoreType.DMA
    return pl.pallas_call(
        kernel,
        out_shape=(
            jax.ShapeDtypeStruct((BS, RB), F32),
            jax.ShapeDtypeStruct((RB, CB), F32),
        ),
        in_specs=[anywhere] * 4 + [vmem],
        out_specs=(vmem, anywhere),
        scratch_shapes=[
            pltpu.VMEM((RB, CB), F32),
            pltpu.VMEM((RB, CB), BF16),
            pltpu.VMEM((RB, CB), BF16),
            pltpu.VMEM((NCOL, RB), F32),
            pltpu.VMEM((BS, RB), F32),
            pltpu.VMEM((STEPS, SEQ, RB), F32),
            pltpu.VMEM((STEPS, RB, SEQ), BF16),
            pltpu.VMEM((STEPS, RB, SEQ), BF16),
            pltpu.VMEM((2, BS, RB), F32),
            pltpu.VMEM((2, BS, RB), F32),
            pltpu.VMEM((BS, RB), F32),
            pltpu.VMEM((STEPS, 2, SEQ, RB), F32),
            pltpu.VMEM((STEPS, C, HALF, RB), F32),
            pltpu.VMEM((STEPS, HALF, RB), F32),
            pltpu.VMEM((STEPS, Z, BS, RB), F32),
            pltpu.VMEM((RB, CB), F32),
            pltpu.VMEM((RB, CB), F32),
            pltpu.VMEM((STEPS, Z, 8, HALF), F32),
            pltpu.VMEM((STEPS, Y, 8, HALF), F32),
            pltpu.VMEM((STEPS, X, 8, HALF), F32),
            pltpu.VMEM((STEPS, C, 8, HALF), F32),
            pltpu.VMEM((STEPS, C, HALF, HALF), F32),
            dma((4,)),
            dma((2,)), dma((2,)),
            dma((Z,)), dma((Z,)),
            dma((2,)),
            dma((STEPS, Y)), dma((STEPS, C, Y)),
            dma((STEPS, 2, C, Y)), dma((STEPS, 2, C, Y)),
            dma((STEPS, C, Y // 2)),
            dma((STEPS,)), dma((STEPS,)),
            dma((STEPS, Z)), dma((STEPS, Z)),
            dma((STEPS, Z)), dma((STEPS, Z)),
            dma((STEPS, Y)), dma((STEPS, Y)),
            dma((STEPS, X)), dma((STEPS, X)),
            dma((STEPS,)), dma((STEPS,)),
            dma((2,)),
        ],
        compiler_params=pltpu.CompilerParams(
            collective_id=0, has_side_effects=True, vmem_limit_bytes=48 * 1024 * 1024
        ),
    )(transition, alphas, beta_last, emission, token_ids)


def solution(mesh):
    return jax.shard_map(
        per_device,
        mesh=mesh,
        in_specs=(
            P("row", "col"),
            P(None, "col", "row"),
            P("col", "row"),
            P(None, "row"),
            P(None, "col"),
        ),
        out_specs=(P("col", "row"), P("row", "col")),
        check_vma=False,
    )
```

time: 561 us -> 106 us (0.19)
  waiting for transfers between devices: 272 us -> 0 us
  blocking collectives: 253 us -> 0 us
  Pallas kernels: 0 us -> 98.6 us
  matrix products: 14 us -> 0 us
  between operations: 13.8 us -> 0.65 us
    all_gather x2 -> x0, waiting for transfers between devices: 171 us -> none  [per_device(): panel = lax.all_gather(weighted, 'row', axis=1, tiled=True)]
    psum x2 -> x0, blocking collectives: 121 us -> none  [per_device(): norms = lax.psum(jnp.sum(alphas[k] * local, axis=1), 'row')]
    reduce_scatter x2 -> x0, waiting for transfers between devices: 100 us -> none  [per_device(): lax.psum_scatter(lax.dot_general(columns, transition, (((1,), (1,)), ((),...]
    pallas_call x0 -> x1, Pallas kernels: none -> 98.6 us  [per_device(): pl.pallas_call(kernel, out_shape=(jax.ShapeDtypeStruct((BS, RB), F32), ja...]
    all_to_all x2 -> x0, blocking collectives: 81.5 us -> none  [per_device(): lax.all_to_all(panel, 'col', split_axis=1, concat_axis=0, tiled=True)]
    all_gather x2 -> x0, blocking collectives: 50.4 us -> none  [per_device(): lax.all_gather(alphas[k] / norms[:, None], 'col', axis=0, tiled=True)]
    dot_general x6 -> x0, matrix products: 14 us -> none  [the longest x2 5.46 us: per_device(): lax.dot_general(columns, transition, (((1,), (1,)), ((), ())), precision=...]
    unnamed x10 -> x12, local copies, waits for them, and re-layouts: 1.12 us -> 6.74 us
  transfers between devices with their start and end apart: 4 -> 0, of which waited for: 4 -> 0; matrix products, arithmetic and copies ran while one was open for 0% -> 0% of each run, Pallas kernels for 0% -> 0%
where the time goes in v1:
time: 106 us
  Pallas kernels  98.6 us (93%)
  local copies, waits for them, and re-layouts  6.74 us (6%)
    pallas_call x1, Pallas kernels, per_device(): pl.pallas_call(kernel, out_shape=(jax.ShapeDtypeStruct((BS, RB), F32), ja...  98.6 us
    unnamed x12, local copies, waits for them, and re-layouts  6.74 us

profile of v1, /device:TPU:1, one launch (start us, length us, event | category | flops | bytes accessed | tf_op | source)
XLA Modules:
  0.0 106.0 jit_solution(3428627409217890025)
XLA Ops:
  0.6 0.0 copy-start
  0.6 1.6 %copy-done = f32[512,1024]{1,0:T(8,128)S(1)} copy-done((f32[512,1024]{1,0:T(8,128)S(1)}, f32[512,1024]{1,0:T(8,128)}, u32[]{:S(2)}) %copy-start) | copy-done | bytes 2097176
  2.2 0.0 copy-start.1
  2.2 0.9 copy-done.1
  3.2 0.0 copy-start.2
  3.2 0.8 copy-done.2
  4.0 0.0 copy-start.3
  4.0 0.8 copy-done.3
  4.8 0.0 copy-start.4
  4.8 0.7 copy-done.4
  5.5 98.6 %shard_map.68 = (f32[16,512]{1,0:T(8,128)S(1)}, f32[512,1024]{1,0:T(8,128)S(1)}) custom-call(f32[512,1024]{1,0:T(8,128)S(1)} %copy-done, f32[2,16,512]{2,1,0:T(8,128)S(1)} %copy-done.2, f32[16,512]{1,0:T(8,128)S(1)} %copy-done.3, f32[128,512]{1,0:T(8,128)S(1)} %copy-done.1, s32[2,16]{1,0:T(2,128)S(1)} %copy-done.4), custom_call_target="tpu_custom_call" | custom-call | tf_op jit(solution)/shard_map/pallas_call | solution.py:433
  104.0 0.6 copy.9
  104.7 1.3 %copy.10 = f32[512,1024]{1,0:T(8,128)} copy(f32[512,1024]{1,0:T(8,128)S(1)} %get-tuple-element.5) | data formatting | bytes 4194304
Async XLA Ops:
  0.6 1.6 %copy-start = (f32[512,1024]{1,0:T(8,128)S(1)}, f32[512,1024]{1,0:T(8,128)}, u32[]{:S(2)}) copy-start(f32[512,1024]{1,0:T(8,128)} %trans_hbm.1) | copy-start | bytes 6291460
  2.2 0.9 copy-start.1
  3.2 0.8 copy-start.2
  4.0 0.8 copy-start.3
  4.8 0.7 copy-start.4

commit v2 on v0

v2 whole, which is shorter than its diff:
```python
import jax
import jax.numpy as jnp
from jax import lax
from jax.experimental import pallas as pl
from jax.experimental.pallas import tpu as pltpu
from jax.sharding import PartitionSpec as P

H = 16384
STEPS = 2
SEQ = 256
X, Y, Z, C = 4, 8, 8, 2
G = 2
BS = SEQ // (Z * C)
T = BS // G
HALF = SEQ // G
RB = H // (X * Y)
CB = H // (Z * C)
NCOL = 128
FACTOR = float(H * H) / float(SEQ * STEPS)
F32 = jnp.float32
BF16 = jnp.bfloat16
MESH = pl.DeviceIdType.MESH
NT = ((1,), (1,))
NN = ((1,), (0,))


def loop(n, body, start=0):
    def step(i, carry):
        body(i)
        return carry

    lax.fori_loop(start, n, step, 0)


def remote(src, dst, send, recv, row, col):
    return pltpu.make_async_remote_copy(
        src_ref=src, dst_ref=dst, send_sem=send, recv_sem=recv, device_id=(row, col), device_id_type=MESH
    )


def wait(ref, sem):
    pltpu.make_async_copy(ref, ref, sem).wait()


def near_first(j):
    return (j % 2) * ((j + 1) // 2) + (1 - j % 2) * (8 - j // 2)


def split(v):
    hi = v.astype(BF16)
    return hi, (v - hi.astype(F32)).astype(BF16)


def dot(a, b, dims):
    return lax.dot_general(a, b, (dims, ((), ())), preferred_element_type=F32)


def kernel(
    trans_hbm, alphas_hbm, beta_hbm, emis_hbm, tok_hbm,
    beta_out, counts_out,
    t_f, t_hi, t_lo, emis, beta0, tok, al, at_hi, at_lo, tsend, tw, wblk, w, ub, pr, cr, zpart, zz, zy, zx, zc,
    ld, t_s, t_r, a_s, a_r, ap, y_s, y_r, x_s, x_r, f_s, p_s, p_r, c_s, c_r, z_s, z_r,
):
    row = lax.axis_index("row")
    col = lax.axis_index("col")
    x, y, z, k = row % X, row // X, col // C, col % C
    kd = x // 2
    slot = x % 2
    q = (x - 2 * k + 4) % 4
    fslot = 1 - slot
    fhalf = q // 2
    fplus = ((q + 1) // 2) % 2
    xp, xm = (x + 1) % X, (x + X - 1) % X
    fx = fplus * xp + (1 - fplus) * xm
    other = z * C + 1 - k

    loads = [
        pltpu.make_async_copy(tok_hbm, tok, ld.at[0]),
        pltpu.make_async_copy(emis_hbm, emis, ld.at[1]),
        pltpu.make_async_copy(beta_hbm, beta0, ld.at[2]),
        pltpu.make_async_copy(alphas_hbm, al.at[:, :, z, k], ld.at[3]),
        pltpu.make_async_copy(trans_hbm, t_f, ld.at[4]),
    ]
    for c in loads:
        c.start()

    bar = pltpu.get_barrier_semaphore()

    def greet(r, c):
        pl.semaphore_signal(bar, inc=1, device_id=(r, c), device_id_type=MESH)

    def greet_lines(d):
        greet(row, ((z + d) % Z) * C + k)
        greet(((y + d) % Y) * X + x, col)
        greet(((y + d) % Y) * X + x, other)

    def greet_x(d):
        greet(y * X + (x + d) % X, col)
        greet(y * X + (x + d) % X, other)

    loop(Z, greet_lines, 1)
    loop(X, greet_x, 1)
    greet(row, other)

    @pl.when(y != z)
    def _():
        def greet_cross(d):
            greet(((y + d) % Y) * X + x, y * C + k)

            @pl.when((z + d) % Z != y)
            def _():
                greet(z * X + x, ((z + d) % Z) * C + k)

        loop(Z, greet_cross, 1)

    loads[0].wait()
    loads[1].wait()
    labels = lax.broadcasted_iota(jnp.int32, (NCOL, BS), 0)
    em = emis[...]

    def emit(step):
        onehot = (labels == tok[step : step + 1, :]).astype(F32)
        out = lax.dot_general(
            onehot, em, (((0,), (0,)), ((), ())), precision=lax.Precision.HIGHEST, preferred_element_type=F32
        )
        return out.reshape(G, T, RB)

    loads[2].wait()
    tsend[0] = emit(0) * beta0[...]
    tsend[1] = emit(1)

    apart = ((y - z + Z) % Z + Z - 1) // Z
    pl.semaphore_wait(bar, 3 * (Z - 1) + 2 * (X - 1) + 1 + apart * (2 * Z - 3))

    def transpose(src, dst, i):
        @pl.when(y != z)
        def _():
            remote(src, dst, t_s.at[i], t_r.at[i], z * X + x, y * C + k).start()

        @pl.when(y == z)
        def _():
            pltpu.make_async_copy(src, dst, t_r.at[i]).start()

    for g in range(G):
        transpose(tsend.at[0, g], tw.at[0, g], g)

    def alpha_step(i):
        if i < 4:
            b = (z - i + Z) % Z
            ref = al.at[:, :, b, k]
            if i:
                wait(ref, a_r.at[b])
            remote(ref, ref, a_s.at[i], a_r.at[b], row, ((z + 1) % Z) * C + k).start()
        if i < 3:
            b = (z + i) % Z
            ref = al.at[:, :, b, k]
            if i:
                wait(ref, a_r.at[b])
            remote(ref, ref, a_s.at[4 + i], a_r.at[b], row, ((z + Z - 1) % Z) * C + k).start()
        if i == 4:
            for b in ((z + 4) % Z, (z + 3) % Z):
                wait(al.at[:, :, b, k], a_r.at[b])
            half = al.at[:, :, :, k]
            remote(half, half, ap.at[0], ap.at[1], row, other).start()

    def y_sends(step, g, src):
        dst = w.at[step, slot, g, y, k]
        recv = y_r.at[step, g, y]

        @pl.when(k == kd)
        def _():
            pltpu.make_async_copy(src, dst, recv).start()

        @pl.when(k != kd)
        def _():
            remote(src, dst, y_s.at[step, g, 1], recv, row, other).start()

        def send(j):
            to = (y + near_first(j)) % Y
            remote(src, dst, y_s.at[step, g, 0], recv, to * X + x, z * C + kd).start()

        loop(Y, send, 1)

    def x_sends(step, g):
        @pl.when(k == kd)
        def _():
            def send(j):
                s = (y + near_first(j)) % Y
                ref = w.at[step, slot, g, s]
                wait(ref, y_r.at[step, g, s])
                for d, to in enumerate((xp, xm)):
                    theirs = ((q + 1 + 2 * d) % 4) // 2
                    on = 1 - (j + theirs) % 2
                    i = on * (j // 2) + (1 - on) * 4
                    remote(ref, ref, x_s.at[step, g, d], x_r.at[step, g, i], y * X + to, col).start()

            loop(Y, send)

    def forwards(step, g):
        def send(i):
            s = (y + near_first(2 * i + fhalf)) % Y
            ref = w.at[step, fslot, g, s]
            wait(ref, x_r.at[step, g, i])
            remote(ref, ref, f_s.at[step, g], x_r.at[step, g, 5], y * X + fx, col).start()

        loop(Y // 2, send)

    def arrivals(step, g):
        wait(w.at[step, fslot, g, pl.ds(0, Y // 2)], x_r.at[step, g, 4])

        @pl.when(k != kd)
        def _():
            wait(w.at[step, slot, g], x_r.at[step, g, 5])

    def product(step, g):
        acc = None
        for sl in range(2):
            hi, lo = split(w[step, sl, g].reshape(HALF, RB))
            cols = slice(sl * RB, (sl + 1) * RB)
            both = dot(jnp.concatenate([hi, lo], axis=0), t_hi[:, cols], NT)
            part = both[:HALF] + both[HALF:] + dot(hi, t_lo[:, cols], NT)
            acc = part if acc is None else acc + part
        ub[step, g] = acc.reshape(Z, C, T, RB)
        remote(ub.at[step, g, :, 1 - k], pr.at[step, g], p_s.at[step, g], p_r.at[step, g], row, other).start()

    def sums_out(step, g):
        wait(pr.at[step, g], p_r.at[step, g])
        u = ub[step, g, :, k] + pr[step, g]
        ub[step, g, :, k] = u
        dst = cr.at[step, g, z]
        recv = c_r.at[step, g]

        def send(j):
            if step == 0:
                s = (y + near_first(j)) % Y
                r, c = s * X + x, y * C + k
            else:
                s = (z + near_first(j)) % Z
                r, c = row, s * C + k
            remote(ub.at[step, g, s, k], dst, c_s.at[step, g, 0], recv, r, c).start()

        loop(Z, send, 1)
        if step == 0:
            src = ub.at[step, g, y, k]

            @pl.when(y != z)
            def _():
                remote(src, dst, c_s.at[step, g, 1], recv, row, y * C + k).start()

            @pl.when(y == z)
            def _():
                pltpu.make_async_copy(src, dst, recv).start()
        else:
            pltpu.make_async_copy(ub.at[step, g, z, k], dst, recv).start()

    def reduced(step, g):
        wait(cr.at[step, g], c_r.at[step, g])
        acc = cr[step, g, 0]
        for i in range(1, Z):
            acc = acc + cr[step, g, i]
        return acc

    def next_weighted(g):
        wblk[g] = reduced(0, g) * tw[1, g]
        y_sends(1, g, wblk.at[g])

    def z_part(step, g):
        prod = (ub[step, g, :, k] * al[step, g, :, k]).reshape(HALF // C, RB)
        part = prod[:, 0:128]
        for i in range(1, RB // 128):
            part = part + prod[:, i * 128 : (i + 1) * 128]
        zpart[step, g] = part

    def z_sum(parts):
        v = parts[0]
        for p in parts[1:]:
            v = v + p
        return v

    def z_first(step):
        part = zpart[step].reshape(SEQ // C, 128)
        zz[step, z] = jnp.broadcast_to(jnp.sum(jnp.transpose(part), axis=0, keepdims=True), (8, SEQ // C))

        def send(d):
            ref = zz.at[step, z]
            remote(ref, ref, z_s.at[step, 0], z_r.at[step, 0], row, ((z + d) % Z) * C + k).start()

        loop(Z, send, 1)

    def z_second(step):
        wait(zz.at[step, pl.ds(0, Z - 1)], z_r.at[step, 0])
        zy[step, y] = z_sum([zz[step, i] for i in range(Z)])

        def send(d):
            ref = zy.at[step, y]
            remote(ref, ref, z_s.at[step, 1], z_r.at[step, 1], ((y + d) % Y) * X + x, col).start()

        loop(Y, send, 1)

    def z_third(step):
        wait(zy.at[step, pl.ds(0, Y - 1)], z_r.at[step, 1])
        zx[step, x * C + k] = z_sum([zy[step, i] for i in range(Y)])
        ref = zx.at[step, x * C + k]

        def send(d):
            remote(ref, ref, z_s.at[step, 2], z_r.at[step, 2], y * X + (x + d) % X, col).start()
            remote(ref, ref, z_s.at[step, 2], z_r.at[step, 2], y * X + (x + d) % X, other).start()

        loop(X, send, 1)
        remote(ref, ref, z_s.at[step, 2], z_r.at[step, 2], row, other).start()

    def z_last(step):
        wait(zx.at[step, pl.ds(0, X * C - 1)], z_r.at[step, 2])
        for c in range(C):
            v = z_sum([zx[step, i * C + c, 0:1, :] for i in range(X)])
            zc[step, :, :, c] = jnp.transpose(jnp.broadcast_to(v, (128, SEQ // C))).reshape(G, Z, T, 128)

    def scaled_columns(step, sl):
        inv = 1.0 / zc[step].reshape(SEQ, 128)
        return split(w[step, sl].reshape(SEQ, RB) * jnp.concatenate([inv] * (RB // 128), axis=1))

    def counts_part(step, sl):
        hi, lo = scaled_columns(step, sl)
        return dot(at_hi[step], hi, NN) + dot(at_lo[step], hi, NN) + dot(at_hi[step], lo, NN)

    def alphas_turned():
        wait(al.at[:, :, :, 1 - k], ap.at[1])
        for step in range(STEPS):
            v = al[step].reshape(SEQ, RB)
            for i in range(RB // 128):
                hi, lo = split(jnp.transpose(v[:, i * 128 : (i + 1) * 128]))
                at_hi[step, i * 128 : (i + 1) * 128, :] = hi
                at_lo[step, i * 128 : (i + 1) * 128, :] = lo

    loads[4].wait()

    def split_rows(i):
        r = pl.ds(pl.multiple_of(i * 64, 64), 64)
        hi, lo = split(t_f[r, :])
        t_hi[r, :] = hi
        t_lo[r, :] = lo

    loop(RB // 64, split_rows)

    for g in range(G):
        wait(tw.at[0, g], t_r.at[g])
        y_sends(0, g, tw.at[0, g])
    transpose(tsend.at[1], tw.at[1], 2)
    loads[3].wait()
    alpha_step(0)
    x_sends(0, 0)
    forwards(0, 0)
    x_sends(0, 1)
    alpha_step(1)
    arrivals(0, 0)
    product(0, 0)
    forwards(0, 1)
    sums_out(0, 0)
    alpha_step(2)
    arrivals(0, 1)
    product(0, 1)
    alpha_step(3)
    sums_out(0, 1)

    wait(tw.at[1], t_r.at[2])
    next_weighted(0)
    alpha_step(4)
    z_part(0, 0)
    z_part(0, 1)
    x_sends(1, 0)
    next_weighted(1)
    forwards(1, 0)
    z_first(0)
    x_sends(1, 1)
    alphas_turned()
    arrivals(1, 0)
    product(1, 0)
    forwards(1, 1)
    sums_out(1, 0)
    z_second(0)
    z_part(1, 0)
    arrivals(1, 1)
    product(1, 1)
    sums_out(1, 1)
    z_part(1, 1)
    z_first(1)

    z_third(0)
    z_last(0)
    z_second(1)
    counts_out[:, :RB] = counts_part(0, 0)
    z_third(1)
    counts_out[:, RB:] = counts_part(0, 1)

    @pl.when(y != z)
    def _():
        wait(tsend.at[0, 0], t_s.at[0])
        wait(tsend.at[0, 1], t_s.at[1])
        wait(tsend.at[1], t_s.at[2])
        for g in range(G):
            wait(wblk.at[g], c_s.at[0, g, 1])

    for step in range(STEPS):
        for g in range(G):
            wait(cr.at[step, g, pl.ds(0, Y - 1)], y_s.at[step, g, 0])
            wait(cr.at[step, g, pl.ds(0, Z - 1)], c_s.at[step, g, 0])
            wait(pr.at[step, g], p_s.at[step, g])
            wait(w.at[step, 0, g, pl.ds(0, Y // 2)], f_s.at[step, g])

            @pl.when(k != kd)
            def _():
                wait(wblk.at[g], y_s.at[step, g, 1])

            @pl.when(k == kd)
            def _():
                wait(w.at[step, 0, g], x_s.at[step, g, 0])
                wait(w.at[step, 0, g], x_s.at[step, g, 1])

        for i in range(3):
            wait(zz.at[step, pl.ds(0, 7)], z_s.at[step, i])
    for i in range(7):
        wait(al.at[:, :, 0, 0], a_s.at[i])
    wait(al.at[:, :, :, 0], ap.at[0])

    z_last(1)
    for sl in range(2):
        cols = slice(sl * RB, (sl + 1) * RB)
        counts_out[:, cols] = (t_f[:, cols] * (counts_out[:, cols] + counts_part(1, sl))) * FACTOR
    for g in range(G):
        norm = zc[1, g, z, k]
        beta_out[g] = (reduced(1, g) / jnp.concatenate([norm] * (RB // 128), axis=1)) * float(H)


def per_device(transition, alphas, beta_last, emission, token_ids):
    hbm = pl.BlockSpec(memory_space=pltpu.HBM)
    vmem = pl.BlockSpec(memory_space=pltpu.VMEM)
    dma = pltpu.SemaphoreType.DMA
    beta, counts = pl.pallas_call(
        kernel,
        out_shape=(
            jax.ShapeDtypeStruct((G, T, RB), F32),
            jax.ShapeDtypeStruct((RB, CB), F32),
        ),
        in_specs=[hbm] * 5,
        out_specs=(vmem, vmem),
        scratch_shapes=[
            pltpu.VMEM((RB, CB), F32),
            pltpu.VMEM((RB, CB), BF16),
            pltpu.VMEM((RB, CB), BF16),
            pltpu.VMEM((NCOL, RB), F32),
            pltpu.VMEM((G, T, RB), F32),
            pltpu.VMEM((STEPS, BS), jnp.int32),
            pltpu.VMEM((STEPS, G, Z, C, T, RB), F32),
            pltpu.VMEM((STEPS, RB, SEQ), BF16),
            pltpu.VMEM((STEPS, RB, SEQ), BF16),
            pltpu.VMEM((2, G, T, RB), F32),
            pltpu.VMEM((2, G, T, RB), F32),
            pltpu.VMEM((G, T, RB), F32),
            pltpu.VMEM((STEPS, 2, G, Z, C, T, RB), F32),
            pltpu.VMEM((STEPS, G, Z, C, T, RB), F32),
            pltpu.VMEM((STEPS, G, Z, T, RB), F32),
            pltpu.VMEM((STEPS, G, Z, T, RB), F32),
            pltpu.VMEM((STEPS, G, HALF // C, 128), F32),
            pltpu.VMEM((STEPS, Z, 8, 128), F32),
            pltpu.VMEM((STEPS, Y, 8, 128), F32),
            pltpu.VMEM((STEPS, X * C, 8, 128), F32),
            pltpu.VMEM((STEPS, G, Z, C, T, 128), F32),
            dma((5,)),
            dma((3,)), dma((3,)),
            dma((7,)), dma((Z,)),
            dma((2,)),
            dma((STEPS, G, 2)), dma((STEPS, G, Y)),
            dma((STEPS, G, 2)), dma((STEPS, G, 6)),
            dma((STEPS, G)),
            dma((STEPS, G)), dma((STEPS, G)),
            dma((STEPS, G, 2)), dma((STEPS, G)),
            dma((STEPS, 3)), dma((STEPS, 3)),
        ],
        compiler_params=pltpu.CompilerParams(
            collective_id=0, has_side_effects=True, vmem_limit_bytes=60 * 1024 * 1024
        ),
    )(
        transition,
        alphas.reshape(STEPS, G, T, RB),
        beta_last.reshape(G, T, RB),
        emission,
        token_ids,
    )
    return beta.reshape(BS, RB), counts


def solution(mesh):
    return jax.shard_map(
        per_device,
        mesh=mesh,
        in_specs=(
            P("row", "col"),
            P(None, "col", "row"),
            P("col", "row"),
            P(None, "row"),
            P(None, "col"),
        ),
        out_specs=(P("col", "row"), P("row", "col")),
        check_vma=False,
    )
```

time: 561 us -> 90.9 us (0.16)
  waiting for transfers between devices: 272 us -> 0 us
  blocking collectives: 253 us -> 0 us
  Pallas kernels: 0 us -> 85.5 us
  matrix products: 14 us -> 0 us
  between operations: 13.8 us -> 0.64 us
    all_gather x2 -> x0, waiting for transfers between devices: 171 us -> none  [per_device(): panel = lax.all_gather(weighted, 'row', axis=1, tiled=True)]
    psum x2 -> x0, blocking collectives: 121 us -> none  [per_device(): norms = lax.psum(jnp.sum(alphas[k] * local, axis=1), 'row')]
    reduce_scatter x2 -> x0, waiting for transfers between devices: 100 us -> none  [per_device(): lax.psum_scatter(lax.dot_general(columns, transition, (((1,), (1,)), ((),...]
    pallas_call x0 -> x1, Pallas kernels: none -> 85.5 us  [per_device(): pl.pallas_call(kernel, out_shape=(jax.ShapeDtypeStruct((G, T, RB), F32),...]
    all_to_all x2 -> x0, blocking collectives: 81.5 us -> none  [per_device(): lax.all_to_all(panel, 'col', split_axis=1, concat_axis=0, tiled=True)]
    all_gather x2 -> x0, blocking collectives: 50.4 us -> none  [per_device(): lax.all_gather(alphas[k] / norms[:, None], 'col', axis=0, tiled=True)]
    dot_general x6 -> x0, matrix products: 14 us -> none  [the longest x2 5.46 us: per_device(): lax.dot_general(columns, transition, (((1,), (1,)), ((), ())), precision=...]
  transfers between devices with their start and end apart: 4 -> 0, of which waited for: 4 -> 0; matrix products, arithmetic and copies ran while one was open for 0% -> 0% of each run, Pallas kernels for 0% -> 0%
where the time goes in v2:
time: 90.9 us; the launch traced here: 90.7 us
  Pallas kernels  85.5 us (94%)
  local copies, waits for them, and re-layouts  4.53 us (5%)
    pallas_call x1, Pallas kernels, per_device(): pl.pallas_call(kernel, out_shape=(jax.ShapeDtypeStruct((G, T, RB), F32),...  85.5 us
    unnamed x2, local copies, waits for them, and re-layouts  4.53 us

profile of v2, /device:TPU:1, one launch (start us, length us, event | category | flops | bytes accessed | tf_op | source)
XLA Modules:
  0.0 90.7 jit_solution(5119062392126863563)
XLA Ops:
  0.6 85.5 %shard_map.68 = (f32[2,8,512]{2,1,0:T(8,128)}, f32[512,1024]{1,0:T(8,128)}) custom-call(f32[512,1024]{1,0:T(8,128)} %trans_hbm.1, f32[2,2,8,512]{3,2,1,0:T(8,128)} %bitcast.3, f32[2,8,512]{2,1,0:T(8,128)} %bitcast.4, f32[128,512]{1,0:T(8,128)} %emis_hbm.1, s32[2,16]{1,0:T(2,128)} %tok_hbm.1), custom_call_target="tpu_custom_call" | custom-call | tf_op jit(solution)/shard_map/pallas_call | solution.py:438
  86.2 1.4 %copy.9 = f32[16,512]{1,0:T(8,128)} copy(f32[16,512]{1,0:T(8,128)} %bitcast.5) | data formatting | bytes 65536
  87.5 3.2 %copy.10 = f32[512,1024]{1,0:T(8,128)} copy(f32[512,1024]{1,0:T(8,128)} %get-tuple-element.9) | data formatting | bytes 4194304

commit v3 on v2

--- a/solution.py
+++ b/solution.py
@@ -58,20 +58,15 @@
 def kernel(
     trans_hbm, alphas_hbm, beta_hbm, emis_hbm, tok_hbm,
     beta_out, counts_out,
-    t_f, t_hi, t_lo, emis, beta0, tok, al, at_hi, at_lo, tsend, tw, wblk, w, ub, pr, cr, zpart, zz, zy, zx, zc,
-    ld, t_s, t_r, a_s, a_r, ap, y_s, y_r, x_s, x_r, f_s, p_s, p_r, c_s, c_r, z_s, z_r,
+    t_f, t_hi, t_lo, emis, beta0, tok, al, at_hi, at_lo, tsend, wblk, w, ub, pr, cr, g1, zpart, zs, zz, zz1, zy, zx, zc,
+    ld, a_s, a_r, ap, y_s, y_r, x_s, x_r, p_s, p_r, c_s, c_r, z_s, z_r,
 ):
     row = lax.axis_index("row")
     col = lax.axis_index("col")
     x, y, z, k = row % X, row // X, col // C, col % C
     kd = x // 2
     slot = x % 2
-    q = (x - 2 * k + 4) % 4
     fslot = 1 - slot
-    fhalf = q // 2
-    fplus = ((q + 1) // 2) % 2
-    xp, xm = (x + 1) % X, (x + X - 1) % X
-    fx = fplus * xp + (1 - fplus) * xm
     other = z * C + 1 - k
 
     loads = [
@@ -89,10 +84,14 @@
     def greet(r, c):
         pl.semaphore_signal(bar, inc=1, device_id=(r, c), device_id_type=MESH)
 
+    owner = 1 - (k + kd) % 2
+    diag = 1 - ((y - z + Z) % Z + Z - 1) // Z
+
     def greet_lines(d):
-        greet(row, ((z + d) % Z) * C + k)
+        greet(row, ((z + d) % Z) * C)
+        greet(row, ((z + d) % Z) * C + 1)
         greet(((y + d) % Y) * X + x, col)
-        greet(((y + d) % Y) * X + x, other)
+        greet(((y + d) % Y) * X + x, y * C + kd)
 
     def greet_x(d):
         greet(y * X + (x + d) % X, col)
@@ -102,16 +101,20 @@
     loop(X, greet_x, 1)
     greet(row, other)
 
-    @pl.when(y != z)
+    @pl.when(owner * diag == 0)
     def _():
-        def greet_cross(d):
-            greet(((y + d) % Y) * X + x, y * C + k)
-
-            @pl.when((z + d) % Z != y)
+        greet(row, y * C + kd)
+
+    @pl.when(owner == 1)
+    def _():
+        def greet_back(d):
+            greet(z * X + x, ((z + d) % Z) * C + 1 - k)
+
+            @pl.when(diag * (Z - d) != Z)
             def _():
                 greet(z * X + x, ((z + d) % Z) * C + k)
 
-        loop(Z, greet_cross, 1)
+        loop(Z, greet_back)
 
     loads[0].wait()
     loads[1].wait()
@@ -129,20 +132,7 @@
     tsend[0] = emit(0) * beta0[...]
     tsend[1] = emit(1)
 
-    apart = ((y - z + Z) % Z + Z - 1) // Z
-    pl.semaphore_wait(bar, 3 * (Z - 1) + 2 * (X - 1) + 1 + apart * (2 * Z - 3))
-
-    def transpose(src, dst, i):
-        @pl.when(y != z)
-        def _():
-            remote(src, dst, t_s.at[i], t_r.at[i], z * X + x, y * C + k).start()
-
-        @pl.when(y == z)
-        def _():
-            pltpu.make_async_copy(src, dst, t_r.at[i]).start()
-
-    for g in range(G):
-        transpose(tsend.at[0, g], tw.at[0, g], g)
+    pl.semaphore_wait(bar, 3 * (Z - 1) + 2 * (X - 1) + 1 + Y + owner * (Z * C - 2 * diag))
 
     def alpha_step(i):
         if i < 4:
@@ -164,53 +154,43 @@
             remote(half, half, ap.at[0], ap.at[1], row, other).start()
 
     def y_sends(step, g, src):
-        dst = w.at[step, slot, g, y, k]
-        recv = y_r.at[step, g, y]
-
-        @pl.when(k == kd)
+        dst = w.at[step, slot, g, z, k]
+        recv = y_r.at[step, g, z]
+
+        @pl.when(owner * diag == 1)
         def _():
             pltpu.make_async_copy(src, dst, recv).start()
 
-        @pl.when(k != kd)
+        @pl.when(owner * diag == 0)
         def _():
-            remote(src, dst, y_s.at[step, g, 1], recv, row, other).start()
+            remote(src, dst, y_s.at[step, g, 1], recv, row, y * C + kd).start()
 
         def send(j):
             to = (y + near_first(j)) % Y
-            remote(src, dst, y_s.at[step, g, 0], recv, to * X + x, z * C + kd).start()
+            remote(src, dst, y_s.at[step, g, 0], recv, to * X + x, y * C + kd).start()
 
         loop(Y, send, 1)
 
     def x_sends(step, g):
-        @pl.when(k == kd)
+        @pl.when(owner == 1)
         def _():
             def send(j):
-                s = (y + near_first(j)) % Y
+                s = (z + near_first(j)) % Z
                 ref = w.at[step, slot, g, s]
                 wait(ref, y_r.at[step, g, s])
-                for d, to in enumerate((xp, xm)):
-                    theirs = ((q + 1 + 2 * d) % 4) // 2
-                    on = 1 - (j + theirs) % 2
-                    i = on * (j // 2) + (1 - on) * 4
-                    remote(ref, ref, x_s.at[step, g, d], x_r.at[step, g, i], y * X + to, col).start()
-
-            loop(Y, send)
-
-    def forwards(step, g):
-        def send(i):
-            s = (y + near_first(2 * i + fhalf)) % Y
-            ref = w.at[step, fslot, g, s]
-            wait(ref, x_r.at[step, g, i])
-            remote(ref, ref, f_s.at[step, g], x_r.at[step, g, 5], y * X + fx, col).start()
-
-        loop(Y // 2, send)
+                for d in (2, 1, 3):
+                    remote(ref, ref, x_s.at[step, g], x_r.at[step, g], y * X + (x + d) % X, col).start()
+
+            loop(Z, send)
 
     def arrivals(step, g):
-        wait(w.at[step, fslot, g, pl.ds(0, Y // 2)], x_r.at[step, g, 4])
-
-        @pl.when(k != kd)
+        @pl.when(owner == 1)
         def _():
-            wait(w.at[step, slot, g], x_r.at[step, g, 5])
+            wait(w.at[step, fslot, g], x_r.at[step, g])
+
+        @pl.when(owner == 0)
+        def _():
+            wait(w.at[step, :, g], x_r.at[step, g])
 
     def product(step, g):
         acc = None
@@ -231,27 +211,11 @@
         recv = c_r.at[step, g]
 
         def send(j):
-            if step == 0:
-                s = (y + near_first(j)) % Y
-                r, c = s * X + x, y * C + k
-            else:
-                s = (z + near_first(j)) % Z
-                r, c = row, s * C + k
-            remote(ub.at[step, g, s, k], dst, c_s.at[step, g, 0], recv, r, c).start()
+            s = (z + near_first(j)) % Z
+            remote(ub.at[step, g, s, k], dst, c_s.at[step, g], recv, row, s * C + k).start()
 
         loop(Z, send, 1)
-        if step == 0:
-            src = ub.at[step, g, y, k]
-
-            @pl.when(y != z)
-            def _():
-                remote(src, dst, c_s.at[step, g, 1], recv, row, y * C + k).start()
-
-            @pl.when(y == z)
-            def _():
-                pltpu.make_async_copy(src, dst, recv).start()
-        else:
-            pltpu.make_async_copy(ub.at[step, g, z, k], dst, recv).start()
+        pltpu.make_async_copy(ub.at[step, g, z, k], dst, recv).start()
 
     def reduced(step, g):
         wait(cr.at[step, g], c_r.at[step, g])
@@ -261,15 +225,53 @@
         return acc
 
     def next_weighted(g):
-        wblk[g] = reduced(0, g) * tw[1, g]
+        wblk[g] = reduced(0, g) * tsend[1, g]
         y_sends(1, g, wblk.at[g])
 
-    def z_part(step, g):
-        prod = (ub[step, g, :, k] * al[step, g, :, k]).reshape(HALF // C, RB)
-        part = prod[:, 0:128]
-        for i in range(1, RB // 128):
-            part = part + prod[:, i * 128 : (i + 1) * 128]
-        zpart[step, g] = part
+    def lanes(parts):
+        acc = None
+        for v in parts:
+            for i in range(RB // 128):
+                t = v[:, i * 128 : (i + 1) * 128]
+                acc = t if acc is None else acc + t
+        return acc
+
+    def z_part_0():
+        v = (ub[0, :, :, k] * al[0, :, :, k]).reshape(SEQ // C, RB)
+        zz[0, z] = z_row(lanes([v]))
+
+    def z_row(part):
+        return jnp.broadcast_to(jnp.sum(jnp.transpose(part), axis=0, keepdims=True), (8, SEQ // C))
+
+    def z_first_0():
+        def send(d):
+            ref = zz.at[0, z]
+            remote(ref, ref, z_s.at[0, 0], z_r.at[0, 0], row, ((z + d) % Z) * C + k).start()
+
+        loop(Z, send, 1)
+
+    def alpha_transition():
+        a_hi, a_lo = split(al[1].reshape(SEQ, RB))
+        for sl in range(2):
+            cols = slice(sl * RB, (sl + 1) * RB)
+            g1[sl] = (
+                dot(a_hi, t_hi[:, cols], NN) + dot(a_lo, t_hi[:, cols], NN) + dot(a_hi, t_lo[:, cols], NN)
+            ).reshape(G, Z, C, T, RB)
+
+    def z_part_1(g):
+        zpart[g] = lanes([(g1[sl, g] * w[1, sl, g]).reshape(HALF, RB) for sl in range(2)]).reshape(Z, C, T, 128)
+
+    def z_first_1():
+        for c in range(C):
+            zs[c] = z_row(zpart[:, :, c].reshape(SEQ // C, 128))
+        zz1[z * C + k] = zs[k]
+
+        def send(d):
+            for c in range(C):
+                remote(zs.at[c], zz1.at[z * C + k], z_s.at[1, 0], z_r.at[1, 0], row, ((z + d) % Z) * C + c).start()
+
+        loop(Z, send, 1)
+        remote(zs.at[1 - k], zz1.at[z * C + k], z_s.at[1, 0], z_r.at[1, 0], row, other).start()
 
     def z_sum(parts):
         v = parts[0]
@@ -277,19 +279,13 @@
             v = v + p
         return v
 
-    def z_first(step):
-        part = zpart[step].reshape(SEQ // C, 128)
-        zz[step, z] = jnp.broadcast_to(jnp.sum(jnp.transpose(part), axis=0, keepdims=True), (8, SEQ // C))
-
-        def send(d):
-            ref = zz.at[step, z]
-            remote(ref, ref, z_s.at[step, 0], z_r.at[step, 0], row, ((z + d) % Z) * C + k).start()
-
-        loop(Z, send, 1)
-
     def z_second(step):
-        wait(zz.at[step, pl.ds(0, Z - 1)], z_r.at[step, 0])
-        zy[step, y] = z_sum([zz[step, i] for i in range(Z)])
+        if step == 0:
+            wait(zz.at[0, pl.ds(0, Z - 1)], z_r.at[0, 0])
+            zy[step, y] = z_sum([zz[0, i] for i in range(Z)])
+        else:
+            wait(zz1.at[pl.ds(0, Z * C - 1)], z_r.at[1, 0])
+            zy[step, y] = z_sum([zz1[i] for i in range(Z * C)])
 
         def send(d):
             ref = zy.at[step, y]
@@ -332,6 +328,11 @@
                 at_hi[step, i * 128 : (i + 1) * 128, :] = hi
                 at_lo[step, i * 128 : (i + 1) * 128, :] = lo
 
+    for g in range(G):
+        y_sends(0, g, tsend.at[0, g])
+    loads[3].wait()
+    alpha_step(0)
+
     loads[4].wait()
 
     def split_rows(i):
@@ -342,19 +343,11 @@
 
     loop(RB // 64, split_rows)
 
-    for g in range(G):
-        wait(tw.at[0, g], t_r.at[g])
-        y_sends(0, g, tw.at[0, g])
-    transpose(tsend.at[1], tw.at[1], 2)
-    loads[3].wait()
-    alpha_step(0)
     x_sends(0, 0)
-    forwards(0, 0)
     x_sends(0, 1)
     alpha_step(1)
     arrivals(0, 0)
     product(0, 0)
-    forwards(0, 1)
     sums_out(0, 0)
     alpha_step(2)
     arrivals(0, 1)
@@ -362,62 +355,51 @@
     alpha_step(3)
     sums_out(0, 1)
 
-    wait(tw.at[1], t_r.at[2])
     next_weighted(0)
     alpha_step(4)
-    z_part(0, 0)
-    z_part(0, 1)
+    z_part_0()
+    z_first_0()
     x_sends(1, 0)
     next_weighted(1)
-    forwards(1, 0)
-    z_first(0)
     x_sends(1, 1)
     alphas_turned()
+    alpha_transition()
+    z_second(0)
     arrivals(1, 0)
     product(1, 0)
-    forwards(1, 1)
+    z_part_1(0)
     sums_out(1, 0)
-    z_second(0)
-    z_part(1, 0)
+    z_third(0)
     arrivals(1, 1)
+    z_part_1(1)
+    z_first_1()
     product(1, 1)
+    z_last(0)
     sums_out(1, 1)
-    z_part(1, 1)
-    z_first(1)
-
-    z_third(0)
-    z_last(0)
+
+    counts_out[:, :RB] = counts_part(0, 0)
     z_second(1)
-    counts_out[:, :RB] = counts_part(0, 0)
+    counts_out[:, RB:] = counts_part(0, 1)
     z_third(1)
-    counts_out[:, RB:] = counts_part(0, 1)
-
-    @pl.when(y != z)
-    def _():
-        wait(tsend.at[0, 0], t_s.at[0])
-        wait(tsend.at[0, 1], t_s.at[1])
-        wait(tsend.at[1], t_s.at[2])
-        for g in range(G):
-            wait(wblk.at[g], c_s.at[0, g, 1])
 
     for step in range(STEPS):
         for g in range(G):
             wait(cr.at[step, g, pl.ds(0, Y - 1)], y_s.at[step, g, 0])
-            wait(cr.at[step, g, pl.ds(0, Z - 1)], c_s.at[step, g, 0])
+            wait(cr.at[step, g, pl.ds(0, Z - 1)], c_s.at[step, g])
             wait(pr.at[step, g], p_s.at[step, g])
-            wait(w.at[step, 0, g, pl.ds(0, Y // 2)], f_s.at[step, g])
-
-            @pl.when(k != kd)
+
+            @pl.when(owner * diag == 0)
             def _():
                 wait(wblk.at[g], y_s.at[step, g, 1])
 
-            @pl.when(k == kd)
+            @pl.when(owner == 1)
             def _():
-                wait(w.at[step, 0, g], x_s.at[step, g, 0])
-                wait(w.at[step, 0, g], x_s.at[step, g, 1])
-
-        for i in range(3):
-            wait(zz.at[step, pl.ds(0, 7)], z_s.at[step, i])
+                for i in range(X - 1):
+                    wait(w.at[step, 0, g], x_s.at[step, g])
+
+        wait(zz1.at[pl.ds(0, (Z - 1, Z * C - 1)[step])], z_s.at[step, 0])
+        wait(zy.at[0, pl.ds(0, Y - 1)], z_s.at[step, 1])
+        wait(zx.at[0, pl.ds(0, X * C - 1)], z_s.at[step, 2])
     for i in range(7):
         wait(al.at[:, :, 0, 0], a_s.at[i])
     wait(al.at[:, :, :, 0], ap.at[0])
@@ -438,8 +420,8 @@
     beta, counts = pl.pallas_call(
         kernel,
         out_shape=(
-            jax.ShapeDtypeStruct((G, T, RB), F32),
-            jax.ShapeDtypeStruct((RB, CB), F32),
+            pltpu.VMEM((G, T, RB), F32),
+            pltpu.VMEM((RB, CB), F32),
         ),
         in_specs=[hbm] * 5,
         out_specs=(vmem, vmem),
@@ -454,30 +436,30 @@
             pltpu.VMEM((STEPS, RB, SEQ), BF16),
             pltpu.VMEM((STEPS, RB, SEQ), BF16),
             pltpu.VMEM((2, G, T, RB), F32),
-            pltpu.VMEM((2, G, T, RB), F32),
             pltpu.VMEM((G, T, RB), F32),
             pltpu.VMEM((STEPS, 2, G, Z, C, T, RB), F32),
             pltpu.VMEM((STEPS, G, Z, C, T, RB), F32),
             pltpu.VMEM((STEPS, G, Z, T, RB), F32),
             pltpu.VMEM((STEPS, G, Z, T, RB), F32),
-            pltpu.VMEM((STEPS, G, HALF // C, 128), F32),
-            pltpu.VMEM((STEPS, Z, 8, 128), F32),
+            pltpu.VMEM((2, G, Z, C, T, RB), F32),
+            pltpu.VMEM((G, Z, C, T, 128), F32),
+            pltpu.VMEM((C, 8, 128), F32),
+            pltpu.VMEM((1, Z, 8, 128), F32),
+            pltpu.VMEM((Z * C, 8, 128), F32),
             pltpu.VMEM((STEPS, Y, 8, 128), F32),
             pltpu.VMEM((STEPS, X * C, 8, 128), F32),
             pltpu.VMEM((STEPS, G, Z, C, T, 128), F32),
             dma((5,)),
-            dma((3,)), dma((3,)),
             dma((7,)), dma((Z,)),
             dma((2,)),
             dma((STEPS, G, 2)), dma((STEPS, G, Y)),
-            dma((STEPS, G, 2)), dma((STEPS, G, 6)),
-            dma((STEPS, G)),
             dma((STEPS, G)), dma((STEPS, G)),
-            dma((STEPS, G, 2)), dma((STEPS, G)),
+            dma((STEPS, G)), dma((STEPS, G)),
+            dma((STEPS, G)), dma((STEPS, G)),
             dma((STEPS, 3)), dma((STEPS, 3)),
         ],
         compiler_params=pltpu.CompilerParams(
-            collective_id=0, has_side_effects=True, vmem_limit_bytes=60 * 1024 * 1024
+            collective_id=0, has_side_effects=True, vmem_limit_bytes=52 * 1024 * 1024
         ),
     )(
         transition,

time: 90.9 us -> 81.3 us (0.89)
  Pallas kernels: 85.5 us -> 78.6 us
  local copies, waits for them, and re-layouts: 4.53 us -> 1.94 us
    pallas_call x1, Pallas kernels: 85.5 us -> 78.6 us  [per_device(): pl.pallas_call(kernel, out_shape=(pltpu.VMEM((G, T, RB), F32), pltpu.VMEM...]
    unnamed x2, local copies, waits for them, and re-layouts: 4.53 us -> 1.94 us
where the time goes in v3:
time: 81.3 us; the launch traced here: 81.1 us
  Pallas kernels  78.6 us (97%)
  local copies, waits for them, and re-layouts  1.94 us (2%)
    pallas_call x1, Pallas kernels, per_device(): pl.pallas_call(kernel, out_shape=(pltpu.VMEM((G, T, RB), F32), pltpu.VMEM...  78.6 us
    unnamed x2, local copies, waits for them, and re-layouts  1.94 us

profile of v3, /device:TPU:1, one launch (start us, length us, event | category | flops | bytes accessed | tf_op | source)
XLA Modules:
  0.0 81.1 jit_solution(11259678533182662432)
XLA Ops:
  0.6 78.6 %shard_map.68 = (f32[2,8,512]{2,1,0:T(8,128)S(1)}, f32[512,1024]{1,0:T(8,128)S(1)}) custom-call(f32[512,1024]{1,0:T(8,128)} %trans_hbm.1, f32[2,2,8,512]{3,2,1,0:T(8,128)} %bitcast.4, f32[2,8,512]{2,1,0:T(8,128)} %bitcast.5, f32[128,512]{1,0:T(8,128)} %emis_hbm.1, s32[2,16]{1,0:T(2,128)} %tok_hbm.1), custom_call_target="tpu_custom_call" | custom-call | tf_op jit(solution)/shard_map/pallas_call | solution.py:420
  79.2 0.6 copy.9
  79.8 1.3 %copy.10 = f32[512,1024]{1,0:T(8,128)} copy(f32[512,1024]{1,0:T(8,128)S(1)} %get-tuple-element.7) | data formatting | bytes 4194304

commit v4 on v3

--- a/solution.py
+++ b/solution.py
@@ -58,8 +58,8 @@
 def kernel(
     trans_hbm, alphas_hbm, beta_hbm, emis_hbm, tok_hbm,
     beta_out, counts_out,
-    t_f, t_hi, t_lo, emis, beta0, tok, al, at_hi, at_lo, tsend, wblk, w, ub, pr, cr, g1, zpart, zs, zz, zz1, zy, zx, zc,
-    ld, a_s, a_r, ap, y_s, y_r, x_s, x_r, p_s, p_r, c_s, c_r, z_s, z_r,
+    t_f, t_hi, t_lo, emis, beta0, tok, al, at, at_hi, at_lo, tsend, wblk, w, w_hi, w_lo, ub, pr, cr, g1, gx, zpart, zz, zz1, zy, zy1, zx, zx1, zc,
+    ld, a_s, a_r, ap, b_s, b_r, g_s, g_r, y_s, y_r, x_s, x_r, p_s, p_r, c_s, c_r, z_s, z_r,
 ):
     row = lax.axis_index("row")
     col = lax.axis_index("col")
@@ -73,7 +73,7 @@
         pltpu.make_async_copy(tok_hbm, tok, ld.at[0]),
         pltpu.make_async_copy(emis_hbm, emis, ld.at[1]),
         pltpu.make_async_copy(beta_hbm, beta0, ld.at[2]),
-        pltpu.make_async_copy(alphas_hbm, al.at[:, :, z, k], ld.at[3]),
+        pltpu.make_async_copy(alphas_hbm, al.at[:, :, k, z], ld.at[3]),
         pltpu.make_async_copy(trans_hbm, t_f, ld.at[4]),
     ]
     for c in loads:
@@ -130,27 +130,39 @@
 
     loads[2].wait()
     tsend[0] = emit(0) * beta0[...]
-    tsend[1] = emit(1)
 
     pl.semaphore_wait(bar, 3 * (Z - 1) + 2 * (X - 1) + 1 + Y + owner * (Z * C - 2 * diag))
+
+    def alpha_1_sends():
+        ref = al.at[1, :, k, z]
+
+        def send(d):
+            remote(ref, ref, b_s.at[0], b_r.at[0], row, ((z + d) % Z) * C + k).start()
+
+        loop(Z, send, 1)
+
+    def alpha_1_on():
+        wait(al.at[1, :, k, pl.ds(0, Z - 1)], b_r.at[0])
+        half = al.at[1, :, k]
+        remote(half, half, b_s.at[1], b_r.at[1], row, other).start()
 
     def alpha_step(i):
         if i < 4:
             b = (z - i + Z) % Z
-            ref = al.at[:, :, b, k]
+            ref = al.at[0, :, k, b]
             if i:
                 wait(ref, a_r.at[b])
             remote(ref, ref, a_s.at[i], a_r.at[b], row, ((z + 1) % Z) * C + k).start()
         if i < 3:
             b = (z + i) % Z
-            ref = al.at[:, :, b, k]
+            ref = al.at[0, :, k, b]
             if i:
                 wait(ref, a_r.at[b])
             remote(ref, ref, a_s.at[4 + i], a_r.at[b], row, ((z + Z - 1) % Z) * C + k).start()
         if i == 4:
             for b in ((z + 4) % Z, (z + 3) % Z):
-                wait(al.at[:, :, b, k], a_r.at[b])
-            half = al.at[:, :, :, k]
+                wait(al.at[0, :, k, b], a_r.at[b])
+            half = al.at[0, :, k]
             remote(half, half, ap.at[0], ap.at[1], row, other).start()
 
     def y_sends(step, g, src):
@@ -171,7 +183,7 @@
 
         loop(Y, send, 1)
 
-    def x_sends(step, g):
+    def x_stage(step, g):
         @pl.when(owner == 1)
         def _():
             def send(j):
@@ -195,27 +207,28 @@
     def product(step, g):
         acc = None
         for sl in range(2):
-            hi, lo = split(w[step, sl, g].reshape(HALF, RB))
+            hi, lo = split(jnp.concatenate([w[step, sl, g, :, c].reshape(HALF // C, RB) for c in range(C)], axis=0))
+            w_hi[step, sl, g * HALF : (g + 1) * HALF, :] = hi
+            w_lo[step, sl, g * HALF : (g + 1) * HALF, :] = lo
             cols = slice(sl * RB, (sl + 1) * RB)
             both = dot(jnp.concatenate([hi, lo], axis=0), t_hi[:, cols], NT)
             part = both[:HALF] + both[HALF:] + dot(hi, t_lo[:, cols], NT)
             acc = part if acc is None else acc + part
-        ub[step, g] = acc.reshape(Z, C, T, RB)
-        remote(ub.at[step, g, :, 1 - k], pr.at[step, g], p_s.at[step, g], p_r.at[step, g], row, other).start()
+        ub[step, g] = acc.reshape(C, Z, T, RB)
+        remote(ub.at[step, g, 1 - k], pr.at[step, g], p_s.at[step, g], p_r.at[step, g], row, other).start()
 
     def sums_out(step, g):
         wait(pr.at[step, g], p_r.at[step, g])
-        u = ub[step, g, :, k] + pr[step, g]
-        ub[step, g, :, k] = u
+        ub[step, g, k] = ub[step, g, k] + pr[step, g]
         dst = cr.at[step, g, z]
         recv = c_r.at[step, g]
 
         def send(j):
             s = (z + near_first(j)) % Z
-            remote(ub.at[step, g, s, k], dst, c_s.at[step, g], recv, row, s * C + k).start()
+            remote(ub.at[step, g, k, s], dst, c_s.at[step, g], recv, row, s * C + k).start()
 
         loop(Z, send, 1)
-        pltpu.make_async_copy(ub.at[step, g, z, k], dst, recv).start()
+        pltpu.make_async_copy(ub.at[step, g, k, z], dst, recv).start()
 
     def reduced(step, g):
         wait(cr.at[step, g], c_r.at[step, g])
@@ -237,7 +250,7 @@
         return acc
 
     def z_part_0():
-        v = (ub[0, :, :, k] * al[0, :, :, k]).reshape(SEQ // C, RB)
+        v = (ub[0, :, k] * al[0, :, k]).reshape(SEQ // C, RB)
         zz[0, z] = z_row(lanes([v]))
 
     def z_row(part):
@@ -251,27 +264,72 @@
         loop(Z, send, 1)
 
     def alpha_transition():
+        wait(al.at[1, :, 1 - k], b_r.at[1])
         a_hi, a_lo = split(al[1].reshape(SEQ, RB))
         for sl in range(2):
             cols = slice(sl * RB, (sl + 1) * RB)
-            g1[sl] = (
-                dot(a_hi, t_hi[:, cols], NN) + dot(a_lo, t_hi[:, cols], NN) + dot(a_hi, t_lo[:, cols], NN)
-            ).reshape(G, Z, C, T, RB)
+            g1[sl] = dot(a_hi, t_hi[:, cols], NN) + dot(a_lo, t_hi[:, cols], NN) + dot(a_hi, t_lo[:, cols], NN)
+
+        for d in (2, 1, 3, 0):
+            to = (x + d) % X
+
+            @pl.when(to // 2 == k)
+            def _():
+                if d:
+                    remote(g1.at[to % 2], gx.at[x], g_s.at[d], g_r.at[0], y * X + to, col).start()
+                else:
+                    pltpu.make_async_copy(g1.at[to % 2], gx.at[x], g_r.at[0]).start()
+
+    def alpha_transition_sum():
+        @pl.when(owner == 1)
+        def _():
+            wait(gx, g_r.at[0])
+            gx[0] = z_sum([gx[i] for i in range(X)])
 
     def z_part_1(g):
-        zpart[g] = lanes([(g1[sl, g] * w[1, sl, g]).reshape(HALF, RB) for sl in range(2)]).reshape(Z, C, T, 128)
+        @pl.when(owner == 1)
+        def _():
+            for c in range(C):
+                a = g * HALF + c * (HALF // C)
+                zpart[c, g] = lanes([gx[0, a : a + HALF // C, :] * w[1, slot, g, :, c].reshape(HALF // C, RB)])
 
     def z_first_1():
-        for c in range(C):
-            zs[c] = z_row(zpart[:, :, c].reshape(SEQ // C, 128))
-        zz1[z * C + k] = zs[k]
-
-        def send(d):
+        @pl.when(owner == 1)
+        def _():
             for c in range(C):
-                remote(zs.at[c], zz1.at[z * C + k], z_s.at[1, 0], z_r.at[1, 0], row, ((z + d) % Z) * C + c).start()
-
-        loop(Z, send, 1)
-        remote(zs.at[1 - k], zz1.at[z * C + k], z_s.at[1, 0], z_r.at[1, 0], row, other).start()
+                zz1[z, c] = z_row(zpart[c].reshape(SEQ // C, 128))
+            ref = zz1.at[z]
+
+            def send(d):
+                remote(ref, ref, z_s.at[1, 0], z_r.at[1, 0], row, ((z + d) % Z) * C + k).start()
+
+            loop(Z, send, 1)
+
+    def z_second_1():
+        @pl.when(owner == 1)
+        def _():
+            wait(zz1.at[pl.ds(0, Z - 1)], z_r.at[1, 0])
+            zy1[y] = z_sum([zz1[i] for i in range(Z)])
+            ref = zy1.at[y]
+
+            def send(d):
+                remote(ref, ref, z_s.at[1, 1], z_r.at[1, 1], ((y + d) % Y) * X + x, col).start()
+
+            loop(Y, send, 1)
+
+    def z_third_1():
+        @pl.when(owner == 1)
+        def _():
+            wait(zy1.at[pl.ds(0, Y - 1)], z_r.at[1, 1])
+            zx1[x] = z_sum([zy1[i] for i in range(Y)])
+            ref = zx1.at[x]
+
+            def send(d):
+                remote(ref, ref, z_s.at[1, 2], z_r.at[1, 2], y * X + (x + d) % X, col).start()
+                remote(ref, ref, z_s.at[1, 2], z_r.at[1, 2], y * X + (x + d) % X, other).start()
+
+            loop(X, send, 1)
+            remote(ref, ref, z_s.at[1, 2], z_r.at[1, 2], row, other).start()
 
     def z_sum(parts):
         v = parts[0]
@@ -279,59 +337,66 @@
             v = v + p
         return v
 
-    def z_second(step):
+    def z_second_0():
+        wait(zz.at[0, pl.ds(0, Z - 1)], z_r.at[0, 0])
+        zy[y] = z_sum([zz[0, i] for i in range(Z)])
+
+        def send(d):
+            ref = zy.at[y]
+            remote(ref, ref, z_s.at[0, 1], z_r.at[0, 1], ((y + d) % Y) * X + x, col).start()
+
+        loop(Y, send, 1)
+
+    def z_third_0():
+        wait(zy.at[pl.ds(0, Y - 1)], z_r.at[0, 1])
+        zx[x * C + k] = z_sum([zy[i] for i in range(Y)])
+        ref = zx.at[x * C + k]
+
+        def send(d):
+            remote(ref, ref, z_s.at[0, 2], z_r.at[0, 2], y * X + (x + d) % X, col).start()
+            remote(ref, ref, z_s.at[0, 2], z_r.at[0, 2], y * X + (x + d) % X, other).start()
+
+        loop(X, send, 1)
+        remote(ref, ref, z_s.at[0, 2], z_r.at[0, 2], row, other).start()
+
+    def z_last(step):
         if step == 0:
-            wait(zz.at[0, pl.ds(0, Z - 1)], z_r.at[0, 0])
-            zy[step, y] = z_sum([zz[0, i] for i in range(Z)])
+            wait(zx.at[pl.ds(0, X * C - 1)], z_r.at[0, 2])
+            sums = [z_sum([zx[i * C + c, 0:1, :] for i in range(X)]) for c in range(C)]
         else:
-            wait(zz1.at[pl.ds(0, Z * C - 1)], z_r.at[1, 0])
-            zy[step, y] = z_sum([zz1[i] for i in range(Z * C)])
-
-        def send(d):
-            ref = zy.at[step, y]
-            remote(ref, ref, z_s.at[step, 1], z_r.at[step, 1], ((y + d) % Y) * X + x, col).start()
-
-        loop(Y, send, 1)
-
-    def z_third(step):
-        wait(zy.at[step, pl.ds(0, Y - 1)], z_r.at[step, 1])
-        zx[step, x * C + k] = z_sum([zy[step, i] for i in range(Y)])
-        ref = zx.at[step, x * C + k]
-
-        def send(d):
-            remote(ref, ref, z_s.at[step, 2], z_r.at[step, 2], y * X + (x + d) % X, col).start()
-            remote(ref, ref, z_s.at[step, 2], z_r.at[step, 2], y * X + (x + d) % X, other).start()
-
-        loop(X, send, 1)
-        remote(ref, ref, z_s.at[step, 2], z_r.at[step, 2], row, other).start()
-
-    def z_last(step):
-        wait(zx.at[step, pl.ds(0, X * C - 1)], z_r.at[step, 2])
-        for c in range(C):
-            v = z_sum([zx[step, i * C + c, 0:1, :] for i in range(X)])
-            zc[step, :, :, c] = jnp.transpose(jnp.broadcast_to(v, (128, SEQ // C))).reshape(G, Z, T, 128)
-
-    def scaled_columns(step, sl):
-        inv = 1.0 / zc[step].reshape(SEQ, 128)
-        return split(w[step, sl].reshape(SEQ, RB) * jnp.concatenate([inv] * (RB // 128), axis=1))
+            @pl.when(owner == 1)
+            def _():
+                wait(zx1.at[pl.ds(0, X - 1)], z_r.at[1, 2])
+
+            @pl.when(owner == 0)
+            def _():
+                wait(zx1, z_r.at[1, 2])
+
+            sums = [z_sum([zx1[i, c, 0:1, :] for i in range(X)]) for c in range(C)]
+        n = HALF // C
+        inv = [1.0 / v for v in sums]
+        scale = jnp.concatenate([v[:, g * n : (g + 1) * n] for g in range(G) for v in inv], axis=1)
+        at_hi[...], at_lo[...] = split(at[step] * scale)
 
     def counts_part(step, sl):
-        hi, lo = scaled_columns(step, sl)
-        return dot(at_hi[step], hi, NN) + dot(at_lo[step], hi, NN) + dot(at_hi[step], lo, NN)
+        return (
+            dot(at_hi[...], w_hi[step, sl], NN)
+            + dot(at_lo[...], w_hi[step, sl], NN)
+            + dot(at_hi[...], w_lo[step, sl], NN)
+        )
 
     def alphas_turned():
-        wait(al.at[:, :, :, 1 - k], ap.at[1])
+        wait(al.at[0, :, 1 - k], ap.at[1])
         for step in range(STEPS):
             v = al[step].reshape(SEQ, RB)
             for i in range(RB // 128):
-                hi, lo = split(jnp.transpose(v[:, i * 128 : (i + 1) * 128]))
-                at_hi[step, i * 128 : (i + 1) * 128, :] = hi
-                at_lo[step, i * 128 : (i + 1) * 128, :] = lo
+                at[step, i * 128 : (i + 1) * 128, :] = jnp.transpose(v[:, i * 128 : (i + 1) * 128])
 
     for g in range(G):
         y_sends(0, g, tsend.at[0, g])
+    tsend[1] = emit(1)
     loads[3].wait()
-    alpha_step(0)
+    alpha_1_sends()
 
     loads[4].wait()
 
@@ -343,44 +408,47 @@
 
     loop(RB // 64, split_rows)
 
-    x_sends(0, 0)
-    x_sends(0, 1)
-    alpha_step(1)
+    x_stage(0, 0)
+    alpha_step(0)
+    x_stage(0, 1)
+    alpha_1_on()
     arrivals(0, 0)
     product(0, 0)
+    alpha_step(1)
     sums_out(0, 0)
-    alpha_step(2)
+    alpha_transition()
     arrivals(0, 1)
     product(0, 1)
+    alpha_step(2)
+    sums_out(0, 1)
+
+    next_weighted(0)
     alpha_step(3)
-    sums_out(0, 1)
-
-    next_weighted(0)
+    x_stage(1, 0)
+    next_weighted(1)
     alpha_step(4)
+    alpha_transition_sum()
+    z_part_1(0)
     z_part_0()
     z_first_0()
-    x_sends(1, 0)
-    next_weighted(1)
-    x_sends(1, 1)
+    x_stage(1, 1)
+    z_part_1(1)
+    z_first_1()
     alphas_turned()
-    alpha_transition()
-    z_second(0)
     arrivals(1, 0)
     product(1, 0)
-    z_part_1(0)
+    z_second_0()
+    z_second_1()
     sums_out(1, 0)
-    z_third(0)
+    z_third_0()
     arrivals(1, 1)
-    z_part_1(1)
-    z_first_1()
     product(1, 1)
+    z_third_1()
+    sums_out(1, 1)
+
     z_last(0)
-    sums_out(1, 1)
-
-    counts_out[:, :RB] = counts_part(0, 0)
-    z_second(1)
-    counts_out[:, RB:] = counts_part(0, 1)
-    z_third(1)
+    for sl in range(2):
+        counts_out[:, sl * RB : (sl + 1) * RB] = counts_part(0, sl)
 
     for step in range(STEPS):
         for g in range(G):
@@ -397,19 +465,36 @@
                 for i in range(X - 1):
                     wait(w.at[step, 0, g], x_s.at[step, g])
 
-        wait(zz1.at[pl.ds(0, (Z - 1, Z * C - 1)[step])], z_s.at[step, 0])
-        wait(zy.at[0, pl.ds(0, Y - 1)], z_s.at[step, 1])
-        wait(zx.at[0, pl.ds(0, X * C - 1)], z_s.at[step, 2])
+    wait(zz.at[0, pl.ds(0, Z - 1)], z_s.at[0, 0])
+    wait(zy.at[pl.ds(0, Y - 1)], z_s.at[0, 1])
+    wait(zx.at[pl.ds(0, X * C - 1)], z_s.at[0, 2])
+
+    @pl.when(owner == 1)
+    def _():
+        wait(zz1.at[pl.ds(0, Z - 1)], z_s.at[1, 0])
+        wait(zy1.at[pl.ds(0, Y - 1)], z_s.at[1, 1])
+        for i in range(X * C - 1):
+            wait(zx1.at[0], z_s.at[1, 2])
+
+    for d in (1, 2, 3):
+        @pl.when(((x + d) % X) // 2 == k)
+        def _():
+            wait(g1.at[0], g_s.at[d])
+
+    wait(al.at[1, :, k, pl.ds(0, Z - 1)], b_s.at[0])
+    wait(al.at[1, :, k], b_s.at[1])
     for i in range(7):
-        wait(al.at[:, :, 0, 0], a_s.at[i])
-    wait(al.at[:, :, :, 0], ap.at[0])
+        wait(al.at[0, :, 0, 0], a_s.at[i])
+    wait(al.at[0, :, 0], ap.at[0])
 
     z_last(1)
     for sl in range(2):
         cols = slice(sl * RB, (sl + 1) * RB)
         counts_out[:, cols] = (t_f[:, cols] * (counts_out[:, cols] + counts_part(1, sl))) * FACTOR
+    own = z_sum([zx1[i, k, 0:1, :] for i in range(X)])
+    zc[...] = jnp.transpose(jnp.broadcast_to(own, (128, SEQ // C))).reshape(G, Z, T, 128)
     for g in range(G):
-        norm = zc[1, g, z, k]
+        norm = zc[g, z]
         beta_out[g] = (reduced(1, g) / jnp.concatenate([norm] * (RB // 128), axis=1)) * float(H)
 
 
@@ -432,26 +517,33 @@
             pltpu.VMEM((NCOL, RB), F32),
             pltpu.VMEM((G, T, RB), F32),
             pltpu.VMEM((STEPS, BS), jnp.int32),
-            pltpu.VMEM((STEPS, G, Z, C, T, RB), F32),
-            pltpu.VMEM((STEPS, RB, SEQ), BF16),
-            pltpu.VMEM((STEPS, RB, SEQ), BF16),
+            pltpu.VMEM((STEPS, G, C, Z, T, RB), F32),
+            pltpu.VMEM((STEPS, RB, SEQ), F32),
+            pltpu.VMEM((RB, SEQ), BF16),
+            pltpu.VMEM((RB, SEQ), BF16),
             pltpu.VMEM((2, G, T, RB), F32),
             pltpu.VMEM((G, T, RB), F32),
             pltpu.VMEM((STEPS, 2, G, Z, C, T, RB), F32),
-            pltpu.VMEM((STEPS, G, Z, C, T, RB), F32),
+            pltpu.VMEM((STEPS, 2, SEQ, RB), BF16),
+            pltpu.VMEM((STEPS, 2, SEQ, RB), BF16),
+            pltpu.VMEM((STEPS, G, C, Z, T, RB), F32),
             pltpu.VMEM((STEPS, G, Z, T, RB), F32),
             pltpu.VMEM((STEPS, G, Z, T, RB), F32),
-            pltpu.VMEM((2, G, Z, C, T, RB), F32),
-            pltpu.VMEM((G, Z, C, T, 128), F32),
-            pltpu.VMEM((C, 8, 128), F32),
+            pltpu.VMEM((2, SEQ, RB), F32),
+            pltpu.VMEM((X, SEQ, RB), F32),
+            pltpu.VMEM((C, G, HALF // C, 128), F32),
             pltpu.VMEM((1, Z, 8, 128), F32),
-            pltpu.VMEM((Z * C, 8, 128), F32),
-            pltpu.VMEM((STEPS, Y, 8, 128), F32),
-            pltpu.VMEM((STEPS, X * C, 8, 128), F32),
-            pltpu.VMEM((STEPS, G, Z, C, T, 128), F32),
+            pltpu.VMEM((Z, C, 8, 128), F32),
+            pltpu.VMEM((Y, 8, 128), F32),
+            pltpu.VMEM((Y, C, 8, 128), F32),
+            pltpu.VMEM((X * C, 8, 128), F32),
+            pltpu.VMEM((X, C, 8, 128), F32),
+            pltpu.VMEM((G, Z, T, 128), F32),
             dma((5,)),
             dma((7,)), dma((Z,)),
             dma((2,)),
+            dma((2,)), dma((2,)),
+            dma((X,)), dma((1,)),
             dma((STEPS, G, 2)), dma((STEPS, G, Y)),
             dma((STEPS, G)), dma((STEPS, G)),
             dma((STEPS, G)), dma((STEPS, G)),

time: 81.3 us -> 73.5 us (0.904); the launches traced: 81.1 us -> 72.3 us
  Pallas kernels: 78.6 us -> 69.8 us
    pallas_call x1, Pallas kernels: 78.6 us -> 69.8 us  [per_device(): pl.pallas_call(kernel, out_shape=(pltpu.VMEM((G, T, RB), F32), pltpu.VMEM...]
where the time goes in v4:
time: 73.5 us; the launch traced here: 72.3 us
  Pallas kernels  69.8 us (95%)
  local copies, waits for them, and re-layouts  1.94 us (3%)
    pallas_call x1, Pallas kernels, per_device(): pl.pallas_call(kernel, out_shape=(pltpu.VMEM((G, T, RB), F32), pltpu.VMEM...  69.8 us
    unnamed x2, local copies, waits for them, and re-layouts  1.94 us

profile of v4, /device:TPU:1, one launch (start us, length us, event | category | flops | bytes accessed | tf_op | source)
XLA Modules:
  0.0 72.3 jit_solution(12034203608860064981)
XLA Ops:
  0.6 69.8 %shard_map.68 = (f32[2,8,512]{2,1,0:T(8,128)S(1)}, f32[512,1024]{1,0:T(8,128)S(1)}) custom-call(f32[512,1024]{1,0:T(8,128)} %trans_hbm.1, f32[2,2,8,512]{3,2,1,0:T(8,128)} %bitcast.4, f32[2,8,512]{2,1,0:T(8,128)} %bitcast.5, f32[128,512]{1,0:T(8,128)} %emis_hbm.1, s32[2,16]{1,0:T(2,128)} %tok_hbm.1), custom_call_target="tpu_custom_call" | custom-call | tf_op jit(solution)/shard_map/pallas_call | solution.py:505
  70.4 0.6 copy.9
  71.0 1.3 %copy.10 = f32[512,1024]{1,0:T(8,128)} copy(f32[512,1024]{1,0:T(8,128)S(1)} %get-tuple-element.7) | data formatting | bytes 4194304

commit v5 on v4

--- a/solution.py
+++ b/solution.py
@@ -58,7 +58,7 @@
 def kernel(
     trans_hbm, alphas_hbm, beta_hbm, emis_hbm, tok_hbm,
     beta_out, counts_out,
-    t_f, t_hi, t_lo, emis, beta0, tok, al, at, at_hi, at_lo, tsend, wblk, w, w_hi, w_lo, ub, pr, cr, g1, gx, zpart, zz, zz1, zy, zy1, zx, zx1, zc,
+    t_f, t_hi, t_lo, emis, beta0, tok, al, at, at_hi, at_lo, tsend, wblk, st, w, w_hi, w_lo, ub, pr, cr, g1, gx, zpart, zz, zy, zx, zc,
     ld, a_s, a_r, ap, b_s, b_r, g_s, g_r, y_s, y_r, x_s, x_r, p_s, p_r, c_s, c_r, z_s, z_r,
 ):
     row = lax.axis_index("row")
@@ -87,34 +87,28 @@
     owner = 1 - (k + kd) % 2
     diag = 1 - ((y - z + Z) % Z + Z - 1) // Z
 
+    def greet_cross(d):
+        greet(((y + d) % Y) * X + x, y * C + k)
+        greet(z * X + x, ((z + d) % Z) * C + k)
+
     def greet_lines(d):
-        greet(row, ((z + d) % Z) * C)
-        greet(row, ((z + d) % Z) * C + 1)
+        greet(row, ((z + d) % Z) * C + k)
         greet(((y + d) % Y) * X + x, col)
-        greet(((y + d) % Y) * X + x, y * C + kd)
 
     def greet_x(d):
         greet(y * X + (x + d) % X, col)
         greet(y * X + (x + d) % X, other)
 
+    loop(Z, greet_cross, 1)
+
+    @pl.when(diag == 0)
+    def _():
+        greet(row, y * C + k)
+        greet(z * X + x, col)
+
     loop(Z, greet_lines, 1)
     loop(X, greet_x, 1)
     greet(row, other)
-
-    @pl.when(owner * diag == 0)
-    def _():
-        greet(row, y * C + kd)
-
-    @pl.when(owner == 1)
-    def _():
-        def greet_back(d):
-            greet(z * X + x, ((z + d) % Z) * C + 1 - k)
-
-            @pl.when(diag * (Z - d) != Z)
-            def _():
-                greet(z * X + x, ((z + d) % Z) * C + k)
-
-        loop(Z, greet_back)
 
     loads[0].wait()
     loads[1].wait()
@@ -131,7 +125,7 @@
     loads[2].wait()
     tsend[0] = emit(0) * beta0[...]
 
-    pl.semaphore_wait(bar, 3 * (Z - 1) + 2 * (X - 1) + 1 + Y + owner * (Z * C - 2 * diag))
+    pl.semaphore_wait(bar, 2 * (Z - 1) + 2 * (X - 1) + 1 + 2 * (Z - diag))
 
     def alpha_1_sends():
         ref = al.at[1, :, k, z]
@@ -166,43 +160,64 @@
             remote(half, half, ap.at[0], ap.at[1], row, other).start()
 
     def y_sends(step, g, src):
-        dst = w.at[step, slot, g, z, k]
         recv = y_r.at[step, g, z]
 
-        @pl.when(owner * diag == 1)
-        def _():
-            pltpu.make_async_copy(src, dst, recv).start()
-
-        @pl.when(owner * diag == 0)
-        def _():
-            remote(src, dst, y_s.at[step, g, 1], recv, row, y * C + kd).start()
-
-        def send(j):
-            to = (y + near_first(j)) % Y
-            remote(src, dst, y_s.at[step, g, 0], recv, to * X + x, y * C + kd).start()
-
-        loop(Y, send, 1)
+        def send_to(dst):
+            def send(j):
+                to = (y + near_first(Y - j)) % Y
+                remote(src, dst, y_s.at[step, g, 0], recv, to * X + x, y * C + k).start()
+
+            loop(Y, send, 1)
+
+            @pl.when(diag == 1)
+            def _():
+                pltpu.make_async_copy(src, dst, recv).start()
+
+            @pl.when(diag == 0)
+            def _():
+                remote(src, dst, y_s.at[step, g, 1], recv, row, y * C + k).start()
+
+        @pl.when(owner == 1)
+        def _():
+            send_to(w.at[step, slot, g, z, k])
+
+        @pl.when(owner == 0)
+        def _():
+            send_to(st.at[step, g, z])
 
     def x_stage(step, g):
-        @pl.when(owner == 1)
-        def _():
+        def sends(here, block):
             def send(j):
                 s = (z + near_first(j)) % Z
-                ref = w.at[step, slot, g, s]
-                wait(ref, y_r.at[step, g, s])
+                src = block(s)
+                dst = w.at[step, slot, g, s, k]
+                wait(src, y_r.at[step, g, s])
                 for d in (2, 1, 3):
-                    remote(ref, ref, x_s.at[step, g], x_r.at[step, g], y * X + (x + d) % X, col).start()
+                    remote(src, dst, x_s.at[step, g], x_r.at[step, g], y * X + (x + d) % X, z * C + kd).start()
+                if here:
+                    remote(src, dst, x_s.at[step, g], x_r.at[step, g], row, other).start()
 
             loop(Z, send)
 
+        @pl.when(owner == 1)
+        def _():
+            sends(False, lambda s: w.at[step, slot, g, s, k])
+
+        @pl.when(owner == 0)
+        def _():
+            sends(True, lambda s: st.at[step, g, s])
+
+    def wait_x(step, g, sem):
+        @pl.when(owner == 1)
+        def _():
+            wait(w.at[step, :, g, pl.ds(0, 3 * Z // 4)], sem)
+
+        @pl.when(owner == 0)
+        def _():
+            wait(w.at[step, :, g], sem)
+
     def arrivals(step, g):
-        @pl.when(owner == 1)
-        def _():
-            wait(w.at[step, fslot, g], x_r.at[step, g])
-
-        @pl.when(owner == 0)
-        def _():
-            wait(w.at[step, :, g], x_r.at[step, g])
+        wait_x(step, g, x_r.at[step, g])
 
     def product(step, g):
         acc = None
@@ -224,7 +239,7 @@
         recv = c_r.at[step, g]
 
         def send(j):
-            s = (z + near_first(j)) % Z
+            s = (z + near_first(Z - j)) % Z
             remote(ub.at[step, g, k, s], dst, c_s.at[step, g], recv, row, s * C + k).start()
 
         loop(Z, send, 1)
@@ -252,84 +267,59 @@
     def z_part_0():
         v = (ub[0, :, k] * al[0, :, k]).reshape(SEQ // C, RB)
         zz[0, z] = z_row(lanes([v]))
+        z_first(0)
 
     def z_row(part):
         return jnp.broadcast_to(jnp.sum(jnp.transpose(part), axis=0, keepdims=True), (8, SEQ // C))
 
-    def z_first_0():
+    def z_first(step):
+        if step:
+            zz[1, z] = z_row(zpart[...].reshape(SEQ // C, 128))
+
         def send(d):
-            ref = zz.at[0, z]
-            remote(ref, ref, z_s.at[0, 0], z_r.at[0, 0], row, ((z + d) % Z) * C + k).start()
+            ref = zz.at[step, z]
+            remote(ref, ref, z_s.at[step, 0], z_r.at[step, 0], row, ((z + d) % Z) * C + k).start()
 
         loop(Z, send, 1)
 
     def alpha_transition():
         wait(al.at[1, :, 1 - k], b_r.at[1])
-        a_hi, a_lo = split(al[1].reshape(SEQ, RB))
+        n = HALF // C
+        a_hi, a_lo = split(
+            jnp.concatenate([al[1, g, c].reshape(n, RB) for c in range(C) for g in range(G)], axis=0)
+        )
         for sl in range(2):
             cols = slice(sl * RB, (sl + 1) * RB)
-            g1[sl] = dot(a_hi, t_hi[:, cols], NN) + dot(a_lo, t_hi[:, cols], NN) + dot(a_hi, t_lo[:, cols], NN)
-
-        for d in (2, 1, 3, 0):
+            v = dot(a_hi, t_hi[:, cols], NN) + dot(a_lo, t_hi[:, cols], NN) + dot(a_hi, t_lo[:, cols], NN)
+            g1[sl] = v.reshape(C, G, n, RB)
+
+        for d in (2, 1, 3):
             to = (x + d) % X
 
             @pl.when(to // 2 == k)
             def _():
-                if d:
-                    remote(g1.at[to % 2], gx.at[x], g_s.at[d], g_r.at[0], y * X + to, col).start()
-                else:
-                    pltpu.make_async_copy(g1.at[to % 2], gx.at[x], g_r.at[0]).start()
+                for c in range(C):
+                    remote(g1.at[to % 2, c], gx.at[x], g_s.at[d, c], g_r.at[0], y * X + to, z * C + c).start()
+
+        @pl.when(owner == 1)
+        def _():
+            pltpu.make_async_copy(g1.at[slot, k], gx.at[x], g_r.at[0]).start()
+            remote(g1.at[slot, 1 - k], gx.at[x], g_s.at[0, 0], g_r.at[0], row, other).start()
 
     def alpha_transition_sum():
+        wait(gx, g_r.at[0])
+        gx[0] = z_sum([gx[i] for i in range(X)])
+
+    def z_part_1(g):
+        n = HALF // C
+
         @pl.when(owner == 1)
         def _():
-            wait(gx, g_r.at[0])
-            gx[0] = z_sum([gx[i] for i in range(X)])
-
-    def z_part_1(g):
-        @pl.when(owner == 1)
-        def _():
-            for c in range(C):
-                a = g * HALF + c * (HALF // C)
-                zpart[c, g] = lanes([gx[0, a : a + HALF // C, :] * w[1, slot, g, :, c].reshape(HALF // C, RB)])
-
-    def z_first_1():
-        @pl.when(owner == 1)
-        def _():
-            for c in range(C):
-                zz1[z, c] = z_row(zpart[c].reshape(SEQ // C, 128))
-            ref = zz1.at[z]
-
-            def send(d):
-                remote(ref, ref, z_s.at[1, 0], z_r.at[1, 0], row, ((z + d) % Z) * C + k).start()
-
-            loop(Z, send, 1)
-
-    def z_second_1():
-        @pl.when(owner == 1)
-        def _():
-            wait(zz1.at[pl.ds(0, Z - 1)], z_r.at[1, 0])
-            zy1[y] = z_sum([zz1[i] for i in range(Z)])
-            ref = zy1.at[y]
-
-            def send(d):
-                remote(ref, ref, z_s.at[1, 1], z_r.at[1, 1], ((y + d) % Y) * X + x, col).start()
-
-            loop(Y, send, 1)
-
-    def z_third_1():
-        @pl.when(owner == 1)
-        def _():
-            wait(zy1.at[pl.ds(0, Y - 1)], z_r.at[1, 1])
-            zx1[x] = z_sum([zy1[i] for i in range(Y)])
-            ref = zx1.at[x]
-
-            def send(d):
-                remote(ref, ref, z_s.at[1, 2], z_r.at[1, 2], y * X + (x + d) % X, col).start()
-                remote(ref, ref, z_s.at[1, 2], z_r.at[1, 2], y * X + (x + d) % X, other).start()
-
-            loop(X, send, 1)
-            remote(ref, ref, z_s.at[1, 2], z_r.at[1, 2], row, other).start()
+            zpart[g] = lanes([gx[0, g] * w[1, slot, g, :, k].reshape(n, RB)])
+
+        @pl.when(owner == 0)
+        def _():
+            zpart[g] = lanes([gx[0, g] * st[1, g].reshape(n, RB)])
 
     def z_sum(parts):
         v = parts[0]
@@ -337,42 +327,31 @@
             v = v + p
         return v
 
-    def z_second_0():
-        wait(zz.at[0, pl.ds(0, Z - 1)], z_r.at[0, 0])
-        zy[y] = z_sum([zz[0, i] for i in range(Z)])
+    def z_second(step):
+        wait(zz.at[step, pl.ds(0, Z - 1)], z_r.at[step, 0])
+        zy[step, y] = z_sum([zz[step, i] for i in range(Z)])
 
         def send(d):
-            ref = zy.at[y]
-            remote(ref, ref, z_s.at[0, 1], z_r.at[0, 1], ((y + d) % Y) * X + x, col).start()
+            ref = zy.at[step, y]
+            remote(ref, ref, z_s.at[step, 1], z_r.at[step, 1], ((y + d) % Y) * X + x, col).start()
 
         loop(Y, send, 1)
 
-    def z_third_0():
-        wait(zy.at[pl.ds(0, Y - 1)], z_r.at[0, 1])
-        zx[x * C + k] = z_sum([zy[i] for i in range(Y)])
-        ref = zx.at[x * C + k]
+    def z_third(step):
+        wait(zy.at[step, pl.ds(0, Y - 1)], z_r.at[step, 1])
+        zx[step, x * C + k] = z_sum([zy[step, i] for i in range(Y)])
+        ref = zx.at[step, x * C + k]
 
         def send(d):
-            remote(ref, ref, z_s.at[0, 2], z_r.at[0, 2], y * X + (x + d) % X, col).start()
-            remote(ref, ref, z_s.at[0, 2], z_r.at[0, 2], y * X + (x + d) % X, other).start()
+            remote(ref, ref, z_s.at[step, 2], z_r.at[step, 2], y * X + (x + d) % X, col).start()
+            remote(ref, ref, z_s.at[step, 2], z_r.at[step, 2], y * X + (x + d) % X, other).start()
 
         loop(X, send, 1)
-        remote(ref, ref, z_s.at[0, 2], z_r.at[0, 2], row, other).start()
+        remote(ref, ref, z_s.at[step, 2], z_r.at[step, 2], row, other).start()
 
     def z_last(step):
-        if step == 0:
-            wait(zx.at[pl.ds(0, X * C - 1)], z_r.at[0, 2])
-            sums = [z_sum([zx[i * C + c, 0:1, :] for i in range(X)]) for c in range(C)]
-        else:
-            @pl.when(owner == 1)
-            def _():
-                wait(zx1.at[pl.ds(0, X - 1)], z_r.at[1, 2])
-
-            @pl.when(owner == 0)
-            def _():
-                wait(zx1, z_r.at[1, 2])
-
-            sums = [z_sum([zx1[i, c, 0:1, :] for i in range(X)]) for c in range(C)]
+        wait(zx.at[step, pl.ds(0, X * C - 1)], z_r.at[step, 2])
+        sums = [z_sum([zx[step, i * C + c, 0:1, :] for i in range(X)]) for c in range(C)]
         n = HALF // C
         inv = [1.0 / v for v in sums]
         scale = jnp.concatenate([v[:, g * n : (g + 1) * n] for g in range(G) for v in inv], axis=1)
@@ -430,20 +409,19 @@
     alpha_transition_sum()
     z_part_1(0)
     z_part_0()
-    z_first_0()
     x_stage(1, 1)
     z_part_1(1)
-    z_first_1()
+    z_first(1)
     alphas_turned()
     arrivals(1, 0)
     product(1, 0)
-    z_second_0()
-    z_second_1()
+    z_second(0)
+    z_second(1)
     sums_out(1, 0)
-    z_third_0()
+    z_third(0)
     arrivals(1, 1)
     product(1, 1)
-    z_third_1()
+    z_third(1)
     sums_out(1, 1)
 
     z_last(0)
@@ -456,30 +434,25 @@
             wait(cr.at[step, g, pl.ds(0, Z - 1)], c_s.at[step, g])
             wait(pr.at[step, g], p_s.at[step, g])
 
-            @pl.when(owner * diag == 0)
+            @pl.when(diag == 0)
             def _():
                 wait(wblk.at[g], y_s.at[step, g, 1])
 
-            @pl.when(owner == 1)
-            def _():
-                for i in range(X - 1):
-                    wait(w.at[step, 0, g], x_s.at[step, g])
-
-    wait(zz.at[0, pl.ds(0, Z - 1)], z_s.at[0, 0])
-    wait(zy.at[pl.ds(0, Y - 1)], z_s.at[0, 1])
-    wait(zx.at[pl.ds(0, X * C - 1)], z_s.at[0, 2])
+            wait_x(step, g, x_s.at[step, g])
+
+        wait(zz.at[0, pl.ds(0, Z - 1)], z_s.at[step, 0])
+        wait(zz.at[0, pl.ds(0, Y - 1)], z_s.at[step, 1])
+        wait(zz.at[0, pl.ds(0, X * C - 1)], z_s.at[step, 2])
+
+    for d in (1, 2, 3):
+        @pl.when(((x + d) % X) // 2 == k)
+        def _():
+            for c in range(C):
+                wait(gx.at[0], g_s.at[d, c])
 
     @pl.when(owner == 1)
     def _():
-        wait(zz1.at[pl.ds(0, Z - 1)], z_s.at[1, 0])
-        wait(zy1.at[pl.ds(0, Y - 1)], z_s.at[1, 1])
-        for i in range(X * C - 1):
-            wait(zx1.at[0], z_s.at[1, 2])
-
-    for d in (1, 2, 3):
-        @pl.when(((x + d) % X) // 2 == k)
-        def _():
-            wait(g1.at[0], g_s.at[d])
+        wait(gx.at[0], g_s.at[0, 0])
 
     wait(al.at[1, :, k, pl.ds(0, Z - 1)], b_s.at[0])
     wait(al.at[1, :, k], b_s.at[1])
@@ -491,7 +464,7 @@
     for sl in range(2):
         cols = slice(sl * RB, (sl + 1) * RB)
         counts_out[:, cols] = (t_f[:, cols] * (counts_out[:, cols] + counts_part(1, sl))) * FACTOR
-    own = z_sum([zx1[i, k, 0:1, :] for i in range(X)])
+    own = z_sum([zx[1, i * C + k, 0:1, :] for i in range(X)])
     zc[...] = jnp.transpose(jnp.broadcast_to(own, (128, SEQ // C))).reshape(G, Z, T, 128)
     for g in range(G):
         norm = zc[g, z]
@@ -523,27 +496,25 @@
             pltpu.VMEM((RB, SEQ), BF16),
             pltpu.VMEM((2, G, T, RB), F32),
             pltpu.VMEM((G, T, RB), F32),
+            pltpu.VMEM((STEPS, G, Z, T, RB), F32),
             pltpu.VMEM((STEPS, 2, G, Z, C, T, RB), F32),
             pltpu.VMEM((STEPS, 2, SEQ, RB), BF16),
             pltpu.VMEM((STEPS, 2, SEQ, RB), BF16),
             pltpu.VMEM((STEPS, G, C, Z, T, RB), F32),
             pltpu.VMEM((STEPS, G, Z, T, RB), F32),
             pltpu.VMEM((STEPS, G, Z, T, RB), F32),
-            pltpu.VMEM((2, SEQ, RB), F32),
-            pltpu.VMEM((X, SEQ, RB), F32),
-            pltpu.VMEM((C, G, HALF // C, 128), F32),
-            pltpu.VMEM((1, Z, 8, 128), F32),
-            pltpu.VMEM((Z, C, 8, 128), F32),
-            pltpu.VMEM((Y, 8, 128), F32),
-            pltpu.VMEM((Y, C, 8, 128), F32),
-            pltpu.VMEM((X * C, 8, 128), F32),
-            pltpu.VMEM((X, C, 8, 128), F32),
+            pltpu.VMEM((2, C, G, HALF // C, RB), F32),
+            pltpu.VMEM((X, G, HALF // C, RB), F32),
+            pltpu.VMEM((G, HALF // C, 128), F32),
+            pltpu.VMEM((STEPS, Z, 8, 128), F32),
+            pltpu.VMEM((STEPS, Y, 8, 128), F32),
+            pltpu.VMEM((STEPS, X * C, 8, 128), F32),
             pltpu.VMEM((G, Z, T, 128), F32),
             dma((5,)),
             dma((7,)), dma((Z,)),
             dma((2,)),
             dma((2,)), dma((2,)),
-            dma((X,)), dma((1,)),
+            dma((X, C)), dma((1,)),
             dma((STEPS, G, 2)), dma((STEPS, G, Y)),
             dma((STEPS, G)), dma((STEPS, G)),
             dma((STEPS, G)), dma((STEPS, G)),

time: 73.5 us -> 70.6 us (0.961); the launches traced: 72.3 us -> 70.5 us
  Pallas kernels: 69.8 us -> 67.9 us
    pallas_call x1, Pallas kernels: 69.8 us -> 67.9 us  [per_device(): pl.pallas_call(kernel, out_shape=(pltpu.VMEM((G, T, RB), F32), pltpu.VMEM...]
where the time goes in v5:
time: 70.6 us; the launch traced here: 70.5 us
  Pallas kernels  67.9 us (96%)
  local copies, waits for them, and re-layouts  1.94 us (3%)
    pallas_call x1, Pallas kernels, per_device(): pl.pallas_call(kernel, out_shape=(pltpu.VMEM((G, T, RB), F32), pltpu.VMEM...  67.9 us
    unnamed x2, local copies, waits for them, and re-layouts  1.94 us

profile of v5, /device:TPU:1, one launch (start us, length us, event | category | flops | bytes accessed | tf_op | source)
XLA Modules:
  0.0 70.5 jit_solution(16771484033782992793)
XLA Ops:
  0.6 67.9 %shard_map.68 = (f32[2,8,512]{2,1,0:T(8,128)S(1)}, f32[512,1024]{1,0:T(8,128)S(1)}) custom-call(f32[512,1024]{1,0:T(8,128)} %trans_hbm.1, f32[2,2,8,512]{3,2,1,0:T(8,128)} %bitcast.4, f32[2,8,512]{2,1,0:T(8,128)} %bitcast.5, f32[128,512]{1,0:T(8,128)} %emis_hbm.1, s32[2,16]{1,0:T(2,128)} %tok_hbm.1), custom_call_target="tpu_custom_call" | custom-call | tf_op jit(solution)/shard_map/pallas_call | solution.py:478
  68.5 0.6 copy.9
  69.1 1.3 %copy.10 = f32[512,1024]{1,0:T(8,128)} copy(f32[512,1024]{1,0:T(8,128)S(1)} %get-tuple-element.7) | data formatting | bytes 4194304

commit v6 on v5

--- a/solution.py
+++ b/solution.py
@@ -69,6 +69,37 @@
     fslot = 1 - slot
     other = z * C + 1 - k
 
+    bar = pltpu.get_barrier_semaphore()
+
+    def greet(r, c):
+        pl.semaphore_signal(bar, inc=1, device_id=(r, c), device_id_type=MESH)
+
+    owner = 1 - (k + kd) % 2
+    diag = 1 - ((y - z + Z) % Z + Z - 1) // Z
+
+    def greet_cross(d):
+        greet(((y + d) % Y) * X + x, y * C + k)
+        greet(z * X + x, ((z + d) % Z) * C + k)
+
+    def greet_lines(d):
+        greet(row, ((z + d) % Z) * C + k)
+        greet(((y + d) % Y) * X + x, col)
+
+    def greet_x(d):
+        greet(y * X + (x + d) % X, col)
+        greet(y * X + (x + d) % X, other)
+
+    loop(Z, greet_cross, 1)
+
+    @pl.when(diag == 0)
+    def _():
+        greet(row, y * C + k)
+        greet(z * X + x, col)
+
+    loop(Z, greet_lines, 1)
+    loop(X, greet_x, 1)
+    greet(row, other)
+
     loads = [
         pltpu.make_async_copy(tok_hbm, tok, ld.at[0]),
         pltpu.make_async_copy(emis_hbm, emis, ld.at[1]),
@@ -78,37 +109,6 @@
     ]
     for c in loads:
         c.start()
-
-    bar = pltpu.get_barrier_semaphore()
-
-    def greet(r, c):
-        pl.semaphore_signal(bar, inc=1, device_id=(r, c), device_id_type=MESH)
-
-    owner = 1 - (k + kd) % 2
-    diag = 1 - ((y - z + Z) % Z + Z - 1) // Z
-
-    def greet_cross(d):
-        greet(((y + d) % Y) * X + x, y * C + k)
-        greet(z * X + x, ((z + d) % Z) * C + k)
-
-    def greet_lines(d):
-        greet(row, ((z + d) % Z) * C + k)
-        greet(((y + d) % Y) * X + x, col)
-
-    def greet_x(d):
-        greet(y * X + (x + d) % X, col)
-        greet(y * X + (x + d) % X, other)
-
-    loop(Z, greet_cross, 1)
-
-    @pl.when(diag == 0)
-    def _():
-        greet(row, y * C + k)
-        greet(z * X + x, col)
-
-    loop(Z, greet_lines, 1)
-    loop(X, greet_x, 1)
-    greet(row, other)
 
     loads[0].wait()
     loads[1].wait()
@@ -185,19 +185,20 @@
         def _():
             send_to(st.at[step, g, z])
 
-    def x_stage(step, g):
+    def x_stage(step, g, start=0, stop=Z // 2):
         def sends(here, block):
             def send(j):
-                s = (z + near_first(j)) % Z
-                src = block(s)
-                dst = w.at[step, slot, g, s, k]
-                wait(src, y_r.at[step, g, s])
+                s = (z // 2 + (j % 2) * ((j + 1) // 2) + (1 - j % 2) * (4 - j // 2)) % 4 * 2
+                for i in range(2):
+                    wait(block(s + i), y_r.at[step, g, s + i])
+                src = block(pl.ds(s, 2))
+                dst = w.at[step, slot, g, pl.ds(s, 2), k]
                 for d in (2, 1, 3):
                     remote(src, dst, x_s.at[step, g], x_r.at[step, g], y * X + (x + d) % X, z * C + kd).start()
                 if here:
                     remote(src, dst, x_s.at[step, g], x_r.at[step, g], row, other).start()
 
-            loop(Z, send)
+            loop(stop, send, start)
 
         @pl.when(owner == 1)
         def _():
@@ -403,26 +404,28 @@
 
     next_weighted(0)
     alpha_step(3)
-    x_stage(1, 0)
+    x_stage(1, 0, 0, 2)
     next_weighted(1)
+    x_stage(1, 0, 2)
     alpha_step(4)
+    z_part_0()
+    x_stage(1, 1, 0, 2)
     alpha_transition_sum()
     z_part_1(0)
-    z_part_0()
-    x_stage(1, 1)
+    x_stage(1, 1, 2)
     z_part_1(1)
     z_first(1)
-    alphas_turned()
+    z_second(0)
     arrivals(1, 0)
     product(1, 0)
-    z_second(0)
+    sums_out(1, 0)
+    alphas_turned()
+    z_third(0)
     z_second(1)
-    sums_out(1, 0)
-    z_third(0)
     arrivals(1, 1)
     product(1, 1)
+    sums_out(1, 1)
     z_third(1)
-    sums_out(1, 1)
 
     z_last(0)
     for sl in range(2):

time: 70.6 us -> 70.2 us (level)
  no operation moved by 1% of the time
where the time goes in v6:
time: 70.2 us; the launch traced here: 70.1 us
  Pallas kernels  67.5 us (96%)
  local copies, waits for them, and re-layouts  1.94 us (3%)
    pallas_call x1, Pallas kernels, per_device(): pl.pallas_call(kernel, out_shape=(pltpu.VMEM((G, T, RB), F32), pltpu.VMEM...  67.5 us
    unnamed x2, local copies, waits for them, and re-layouts  1.94 us

profile of v6, /device:TPU:1, one launch (start us, length us, event | category | flops | bytes accessed | tf_op | source)
XLA Modules:
  0.0 70.1 jit_solution(6634129234774505861)
XLA Ops:
  0.6 67.5 %shard_map.68 = (f32[2,8,512]{2,1,0:T(8,128)S(1)}, f32[512,1024]{1,0:T(8,128)S(1)}) custom-call(f32[512,1024]{1,0:T(8,128)} %trans_hbm.1, f32[2,2,8,512]{3,2,1,0:T(8,128)} %bitcast.4, f32[2,8,512]{2,1,0:T(8,128)} %bitcast.5, f32[128,512]{1,0:T(8,128)} %emis_hbm.1, s32[2,16]{1,0:T(2,128)} %tok_hbm.1), custom_call_target="tpu_custom_call" | custom-call | tf_op jit(solution)/shard_map/pallas_call | solution.py:481
  68.1 0.6 copy.9
  68.7 1.3 %copy.10 = f32[512,1024]{1,0:T(8,128)} copy(f32[512,1024]{1,0:T(8,128)S(1)} %get-tuple-element.7) | data formatting | bytes 4194304

commit v7 on v6

--- a/solution.py
+++ b/solution.py
@@ -130,8 +130,8 @@
     def alpha_1_sends():
         ref = al.at[1, :, k, z]
 
-        def send(d):
-            remote(ref, ref, b_s.at[0], b_r.at[0], row, ((z + d) % Z) * C + k).start()
+        def send(j):
+            remote(ref, ref, b_s.at[0], b_r.at[0], row, ((z + near_first(Z - j)) % Z) * C + k).start()
 
         loop(Z, send, 1)
 
@@ -374,9 +374,9 @@
 
     for g in range(G):
         y_sends(0, g, tsend.at[0, g])
-    tsend[1] = emit(1)
     loads[3].wait()
     alpha_1_sends()
+    tsend[1] = emit(1)
 
     loads[4].wait()
 

time: 70.2 us -> 70.4 us (level)
  no operation moved by 1% of the time
where the time goes in v7:
time: 70.4 us; the launch traced here: 70.3 us
  Pallas kernels  67.7 us (96%)
  local copies, waits for them, and re-layouts  1.94 us (3%)
    pallas_call x1, Pallas kernels, per_device(): pl.pallas_call(kernel, out_shape=(pltpu.VMEM((G, T, RB), F32), pltpu.VMEM...  67.7 us
    unnamed x2, local copies, waits for them, and re-layouts  1.94 us

profile of v7, /device:TPU:1, one launch (start us, length us, event | category | flops | bytes accessed | tf_op | source)
XLA Modules:
  0.0 70.3 jit_solution(2006040689099696526)
XLA Ops:
  0.6 67.7 %shard_map.68 = (f32[2,8,512]{2,1,0:T(8,128)S(1)}, f32[512,1024]{1,0:T(8,128)S(1)}) custom-call(f32[512,1024]{1,0:T(8,128)} %trans_hbm.1, f32[2,2,8,512]{3,2,1,0:T(8,128)} %bitcast.4, f32[2,8,512]{2,1,0:T(8,128)} %bitcast.5, f32[128,512]{1,0:T(8,128)} %emis_hbm.1, s32[2,16]{1,0:T(2,128)} %tok_hbm.1), custom_call_target="tpu_custom_call" | custom-call | tf_op jit(solution)/shard_map/pallas_call | solution.py:481
  68.3 0.6 copy.9
  69.0 1.3 %copy.10 = f32[512,1024]{1,0:T(8,128)} copy(f32[512,1024]{1,0:T(8,128)S(1)} %get-tuple-element.7) | data formatting | bytes 4194304
